TPU v7x, 128 devices: a whole 4x4x4 slice. The times are simulated.
128 devices in a mesh: grp: 2 (over core), dp: 64 (over x, y, z).
Axes of the slice: x: 4, y: 4, z: 4, core: 2. Of those that a mesh axis runs over, the one named last changes fastest.
Arguments:
- tokens: bfloat16 [2, 64, 576, 768], P('grp', 'dp'), may hold values from -6 to 6
- cotangent: bfloat16 [2, 64, 576, 768], P('grp', 'dp'), may hold values from -6 to 6
- counts: int32 [2, 64, 2], P('grp', 'dp'), may hold values from 0 to 576, as said below
- patch_row: int32 [2, 64, 576], P('grp', 'dp'), may hold values from 0 to 23, as said below
- patch_col: int32 [2, 64, 576], P('grp', 'dp'), may hold values from 0 to 23, as said below
- w_qkv: float32 [768, 2304], P('dp'), may hold values from -0.21650635 to 0.21650635
- w_proj: float32 [768, 768], P('dp'), may hold values from -4 to 4
- w_fc1: float32 [768, 3072], P('dp'), may hold values from -0.21875 to 0.21875
- w_fc2: float32 [3072, 768], P('dp'), may hold values from -0.109375 to 0.109375
- vectors: float32 [14, 768], P(None, 'dp')
- m_qkv: float32 [768, 2304], P('dp'), may hold values from -0.00061035156 to 0.00061035156
- v_qkv: float32 [768, 2304], P('dp'), may hold values from 8.182106e-09 to 3.244628e-08
- m_proj: float32 [768, 768], P('dp'), may hold values from -6.1035156e-05 to 6.1035156e-05
- v_proj: float32 [768, 768], P('dp'), may hold values from 9.02853e-11 to 3.5267697e-10
- m_fc1: float32 [768, 3072], P('dp'), may hold values from -3.8146973e-05 to 3.8146973e-05
- v_fc1: float32 [768, 3072], P('dp'), may hold values from 3.808911e-11 to 1.4953504e-10
- m_fc2: float32 [3072, 768], P('dp'), may hold values from -7.6293945e-05 to 7.6293945e-05
- v_fc2: float32 [3072, 768], P('dp'), may hold values from 1.4107078e-10 to 5.5017607e-10
- m_vectors: float32 [14, 768], P(None, 'dp'), may hold values from -0.0024414062 to 0.0024414062
- v_vectors: float32 [14, 768], P(None, 'dp'), may hold values from 1.1849946e-07 to 4.796407e-07
Outputs:
- mixed_out: bfloat16 [2, 64, 576, 768], P('grp', 'dp')
- grad_tokens: float32 [2, 64, 576, 768], P('grp', 'dp')
- grad_norm: float32 [], replicated
- qkv_new: float32 [768, 2304], P('dp')
- qkv_first: float32 [768, 2304], P('dp')
- qkv_second: float32 [768, 2304], P('dp')
- proj_new: float32 [768, 768], P('dp')
- proj_first: float32 [768, 768], P('dp')
- proj_second: float32 [768, 768], P('dp')
- fc1_new: float32 [768, 3072], P('dp')
- fc1_first: float32 [768, 3072], P('dp')
- fc1_second: float32 [768, 3072], P('dp')
- fc2_new: float32 [3072, 768], P('dp')
- fc2_first: float32 [3072, 768], P('dp')
- fc2_second: float32 [3072, 768], P('dp')
- vectors_new: float32 [14, 768], P(None, 'dp')
- vectors_first: float32 [14, 768], P(None, 'dp')
- vectors_second: float32 [14, 768], P(None, 'dp')
- bias_proj_grad: float32 [768], P('dp')
Inputs may be any that keep to these rules, and one draw needn't show every extreme that they name: counts[0, f, i] is the number of kept patches of image i of a first-group frame, 98 to 196; counts[1, f, 0] that of the one image of a second-group frame, 288 to 576; counts[1, f, 1] is 0. Kept patches fill their image's first slots. `patch_row`: the kept patches of one image sit at distinct grid positions (rows below 14 in the first group, 24 in the second); other slots hold any position. `patch_col`: column of the same positions.
All inputs are finite; a program needn't handle non-finite values.
Results may differ from a plain program's by a relative error of at most 0.023.
The roundings to bfloat16 on the way count: a program that leaves them out, or rounds other values in their place, can miss the bound.
Values may be sent and summed in bfloat16 or wider, within the bound.
No kernel may reach another device: no remote copies, remote signals or barrier semaphores. Data moves between devices by JAX's collectives and lax.ppermute only.
A program may use at most 192 MiB of HBM per device.

v0:
```python
import jax
import jax.numpy as jnp
from jax import lax
from jax.experimental import pallas as pl
from jax.experimental.pallas import tpu as pltpu
from jax.sharding import PartitionSpec as P

D = 768
H = 12
HD = 64
FF = 3072
STEP = 10
A = 196
S = 576

CORES = 2
HC = H // CORES
DC = D // CORES
FC = FF // CORES
PAIRS = HC // 2
T = CORES * S

WIN = 208
WINDOWS = (0, 192)

EPS_NORM = 1e-06
BETA_ONE = 0.9
BETA_TWO = 0.95
ADAM_EPS = 1e-08
DECAY_RATE = 0.05
RATE_VECTOR = 0.8
CLIP_LIMIT = 1.0
NEG = -1e30

bf16 = jnp.bfloat16
f32 = jnp.float32
VMEM_LIMIT = 56 * 1024 * 1024


SIDE = 4
CHIPS = SIDE**3
PLANE = SIDE * SIDE
KR = D // CHIPS
FR = FC // CHIPS
BLOCK = SIDE * KR
QUARTER = PLANE * KR
BOTH = ("grp", "dp")


def device(core, x, y, z):
    return ((core * SIDE + x) * SIDE + y) * SIDE + z


def lines():
    r = range(SIDE)
    return [[device(0, a, g, z) for a in r] for g in r for z in r] + [
        [device(1, g, a, z) for a in r] for g in r for z in r
    ]


def planes():
    r = range(SIDE)
    return [[device(0, a, g, z) for g in r for z in r] for a in r] + [
        [device(1, g, a, z) for g in r for z in r] for a in r
    ]


def shift(value, d):
    pairs = [(group[i], group[(i + d) % SIDE]) for group in lines() for i in range(SIDE)]
    return lax.ppermute(value, BOTH, pairs)


def plane_swap(value):
    return lax.all_to_all(value, BOTH, 0, 0, axis_index_groups=planes())


def natural(core, a, g):
    return jnp.where(core == 0, SIDE * a + g, SIDE * g + a)


def lay_out(place_ref, pieces, full_ref):
    core, me = place_ref[0], place_ref[1]
    for d, piece in enumerate(pieces):
        a = (me + SIDE - d) & (SIDE - 1)
        for g in range(SIDE):
            at = pl.multiple_of(natural(core, a, g) * BLOCK, BLOCK)
            full_ref[pl.ds(at, BLOCK), :] = piece[g * BLOCK : (g + 1) * BLOCK, :]


def usable_rows(place_ref, group, rows, base=0):
    slot = lax.broadcasted_iota(jnp.int32, (rows, 1), 0) + base
    first = ((slot < A) & (slot < place_ref[2])) | ((slot >= A) & (slot < 2 * A) & (slot - A < place_ref[3]))
    first = first.astype(f32)
    second = (slot < place_ref[4]).astype(f32)
    if isinstance(group, int):
        return second if group else first
    return jnp.where(group == 0, first, second)


def own_rows(win):
    row = lax.broadcasted_iota(jnp.int32, (WIN, 1), 0) + (WINDOWS[win] - win * A)
    return ((row >= 0) & (row < A)).astype(f32)


def key_bias(place_ref, win=None):
    if win is None:
        key = lax.broadcasted_iota(jnp.int32, (1, S), 1)
        return jnp.where(key < place_ref[4], 0.0, NEG)
    key = lax.broadcasted_iota(jnp.int32, (1, WIN), 1) + (WINDOWS[win] - win * A)
    return jnp.where((key >= 0) & (key < place_ref[2 + win]), 0.0, NEG)


def exact_dot(a, b):
    high = a.astype(bf16)
    rest = a - high.astype(f32)
    mid = rest.astype(bf16)
    low = (rest - mid.astype(f32)).astype(bf16)
    b = b.astype(bf16)
    return dot(high, b) + dot(mid, b) + dot(low, b)


def spots(core, shape, full, part):
    l = lax.broadcasted_iota(jnp.int32, shape, full)
    m = lax.broadcasted_iota(jnp.int32, shape, part)
    q = (m * 2731) >> 16
    return l == m + FR * (q + core)


def spots_t(core):
    return spots(core, (DC, D), 1, 0)


def params(**kw):
    return pltpu.CompilerParams(vmem_limit_bytes=VMEM_LIMIT, **kw)


def cost(flops, bytes_accessed, transcendentals=0):
    return pl.CostEstimate(
        flops=int(flops), bytes_accessed=int(bytes_accessed), transcendentals=int(transcendentals)
    )


def dot(a, b):
    return jnp.dot(a, b, preferred_element_type=f32)


def dot_t(a, b):
    return lax.dot_general(a, b, (((1,), (1,)), ((), ())), preferred_element_type=f32)


def t_dot(a, b):
    return lax.dot_general(a, b, (((0,), (0,)), ((), ())), preferred_element_type=f32)


def stats(z):
    mean_val = jnp.mean(z, axis=-1, keepdims=True)
    centred = z - mean_val
    variance = jnp.mean(centred * centred, axis=-1, keepdims=True)
    inv_std = lax.rsqrt(variance + EPS_NORM)
    return centred * inv_std, inv_std


def norm_back(grad, normed, inv_std, gain):
    e = grad * gain
    return inv_std * (
        e
        - jnp.mean(e, axis=-1, keepdims=True)
        - normed * jnp.mean(e * normed, axis=-1, keepdims=True)
    )


def swap_halves(u):
    lanes = u.shape[1]
    lane = lax.broadcasted_iota(jnp.int32, u.shape, 1)
    up = pltpu.roll(u, lanes - HD // 2, 1)
    down = pltpu.roll(u, HD // 2, 1)
    return jnp.where((lane & (HD - 1)) < HD // 2, up, down)


TURN = 1.5707963267948966


def sin_cos(a):
    k = jnp.floor(a * (1.0 / TURN) + 0.5)
    r = ((a - k * 1.5703125) - k * 4.837512969970703125e-4) - k * 7.54978995489188216e-8
    z = r * r
    s = ((-1.9515295891e-4 * z + 8.3321608736e-3) * z - 1.6666654611e-1) * z * r + r
    c = ((2.443315711809948e-5 * z - 1.388731625493765e-3) * z + 4.166664568298827e-2) * z * z - 0.5 * z + 1.0
    quarter = k.astype(jnp.int32)
    odd = (quarter & 1) == 1
    sine = jnp.where(odd, c, s)
    cosine = jnp.where(odd, s, c)
    sine = jnp.where((quarter & 2) == 0, sine, -sine)
    cosine = jnp.where(((quarter + 1) & 2) == 0, cosine, -cosine)
    return sine, cosine


def pre_kernel(
    place_ref, x_ref, xo_ref, c_ref, co_ref, ints_ref, v0, v1, v2, v3,
    vec_ref, h_ref, ht_ref, cos_ref, sin_ref, gy_ref, b1_ref, pos_ref,
    full_s, rows_s,
):
    i = pl.program_id(0)
    core = place_ref[0]

    @pl.when(i == 0)
    def _():
        lay_out(place_ref, (v0, v1, v2, v3), full_s)
        rows_s[...] = full_s[...].astype(f32).T[:16, :]
        vec_ref[...] = rows_s[...]
        units = dot(rows_s[8:16, :].astype(bf16), spots(core, (D, DC), 0, 1).astype(bf16))
        for r in range(FC // DC):
            b1_ref[:, r * DC : (r + 1) * DC] = units[2 + r : 3 + r, :]

    mine = i == 0
    normed, _ = stats(jnp.where(mine, x_ref[...], xo_ref[...]).astype(f32))
    h = normed * rows_s[0:1, :] + rows_s[1:2, :]
    h_ref[...] = h.astype(bf16)
    ht_ref[0] = h.T.astype(bf16)
    keep = usable_rows(place_ref, i ^ core, S)
    gy_ref[...] = (jnp.where(mine, c_ref[...], co_ref[...]).astype(f32) * keep).astype(bf16)
    src = lax.broadcasted_iota(jnp.int32, (D, DC), 0)
    dst = lax.broadcasted_iota(jnp.int32, (D, DC), 1)
    want = core * (DC // 2) + (dst // HD) * (HD // 2) + (dst & (HD // 2 - 1))
    freqs = rows_s[8:16, :].astype(bf16)
    col = dot(freqs, (src == want).astype(bf16))[1:2, :]
    row = dot(freqs, (src == want + D // 2).astype(bf16))[1:2, :]
    pos = ints_ref[0].astype(f32).T
    pos_ref[0] = pos
    angle = pos[:, 1:2] * col + pos[:, 0:1] * row
    lane = lax.broadcasted_iota(jnp.int32, (1, DC), 1)
    sign = jnp.where((lane & (HD - 1)) < HD // 2, -1.0, 1.0)
    small = jnp.max(jnp.abs(angle)) < 8000.0

    @pl.when(small)
    def _():
        sine, cosine = sin_cos(angle)
        cos_ref[...] = cosine
        sin_ref[...] = sine * sign

    @pl.when(jnp.logical_not(small))
    def _():
        cos_ref[...] = jnp.cos(angle)
        sin_ref[...] = jnp.sin(angle) * sign


def pre_call(place, x, xo, c, co, ints, pieces):
    tile = lambda n: pl.BlockSpec((S, n), lambda i, c: (i, 0))
    whole = lambda a: pl.BlockSpec(a.shape, lambda i, c: (0,) * a.ndim)
    return pl.pallas_call(
        pre_kernel,
        grid_spec=pltpu.PrefetchScalarGridSpec(
            num_scalar_prefetch=1,
            grid=(CORES,),
            in_specs=[whole(a) for a in (x, xo, c, co)]
            + [pl.BlockSpec((1, 8, S), lambda i, c: (i, 0, 0))]
            + [whole(a) for a in pieces],
            out_specs=[
                pl.BlockSpec((16, D), lambda i, c: (0, 0)),
                tile(D),
                pl.BlockSpec((1, D, S), lambda i, c: (i, 0, 0)),
                tile(DC),
                tile(DC),
                tile(D),
                pl.BlockSpec((1, FC), lambda i, c: (0, 0)),
                pl.BlockSpec((1, S, 8), lambda i, c: (i, 0, 0)),
            ],
            scratch_shapes=[pltpu.VMEM((D, 128), bf16), pltpu.VMEM((16, D), f32)],
        ),
        out_shape=[
            jax.ShapeDtypeStruct((16, D), f32),
            jax.ShapeDtypeStruct((T, D), bf16),
            jax.ShapeDtypeStruct((CORES, D, S), bf16),
            jax.ShapeDtypeStruct((T, DC), f32),
            jax.ShapeDtypeStruct((T, DC), f32),
            jax.ShapeDtypeStruct((T, D), bf16),
            jax.ShapeDtypeStruct((1, FC), f32),
            jax.ShapeDtypeStruct((CORES, S, 8), f32),
        ],
        compiler_params=params(),
        cost_estimate=cost(T * (20 * D + 40 * DC), T * (D * 10 + DC * 8)),
    )(place, x, xo, c, co, ints, *pieces)


def qkv_kernel(place_ref, h_ref, w0, w1, w2, w3, v_ref, cos_ref, sin_ref, q_out, k_out, v_out, w_s):
    @pl.when(pl.program_id(0) == 0)
    def _():
        lay_out(place_ref, (w0, w1, w2, w3), w_s)

    cosine = cos_ref[...]
    sine = sin_ref[...]
    at = pl.ds(pl.multiple_of(place_ref[0] * DC, DC), DC)
    acc = dot(h_ref[...], w_s[...])
    part = lambda i: jnp.concatenate([acc[:, (3 * p + i) * 128 : (3 * p + i + 1) * 128] for p in range(PAIRS)], axis=1)
    q = part(0) + v_ref[4:5, at]
    k = part(1) + v_ref[5:6, at]
    q_out[...] = ((q * cosine + swap_halves(q) * sine) * HD ** (-0.5)).astype(bf16)
    k_out[...] = (k * cosine + swap_halves(k) * sine).astype(bf16)
    v_out[...] = (part(2) + v_ref[6:7, at]).astype(bf16)


def qkv_call(place, h1, pieces, vec, cosine, sine):
    rows = 288
    tile = lambda n: pl.BlockSpec((rows, n), lambda i, c: (i, 0))
    whole = lambda a: pl.BlockSpec(a.shape, lambda i, c: (0,) * a.ndim)
    return pl.pallas_call(
        qkv_kernel,
        grid_spec=pltpu.PrefetchScalarGridSpec(
            num_scalar_prefetch=1,
            grid=(T // rows,),
            in_specs=[tile(D)] + [whole(a) for a in pieces] + [whole(vec), tile(DC), tile(DC)],
            out_specs=[tile(DC)] * 3,
            scratch_shapes=[pltpu.VMEM((D, 3 * DC), bf16)],
        ),
        out_shape=[jax.ShapeDtypeStruct((T, DC), bf16)] * 3,
        compiler_params=params(),
        cost_estimate=cost(2 * T * D * 3 * DC, T * D * 2 + D * 3 * DC * 2 + T * DC * 14),
    )(place, h1, *pieces, vec, cosine, sine)


def softmax_head(q, k, v, mine, bias):
    s = dot_t(jnp.where(mine, q, jnp.zeros_like(q)), k) + bias
    e = jnp.exp(s - jnp.max(s, axis=-1, keepdims=True))
    p = e * (1.0 / jnp.sum(e, axis=-1, keepdims=True))
    return p


def attn_fwd_kernel(
    place_ref, q0, k0, v0, q1, k1, v1, o_ref, p0_ref, p1_ref
):
    lane = lax.broadcasted_iota(jnp.int32, (1, 2 * HD), 1)
    low = lane < HD
    q, k, v = q1[0], k1[0], v1[0]
    mixes = []
    bias = key_bias(place_ref)
    for head, mine in ((0, low), (1, ~low)):
        p = softmax_head(q, k, v, mine, bias).astype(bf16)
        p1_ref[head] = p
        mixes.append(dot(p, v))
    mix = jnp.where(low, mixes[0], mixes[1])
    o_ref[1] = jnp.where(usable_rows(place_ref, 1, S) > 0, mix, v.astype(f32)).astype(bf16)
    o_ref[0] = v0[0]
    for win, base in enumerate(WINDOWS):
        q, k, v = (r[0, base : base + WIN, :] for r in (q0, k0, v0))
        own = own_rows(win)
        bias = key_bias(place_ref, win)
        mixes = []
        for head, mine in ((0, low), (1, ~low)):
            p = softmax_head(q, k, v, mine, bias)
            p = (p * own).astype(bf16)
            p0_ref[head, win] = p
            mixes.append(dot(p, v))
        mix = jnp.where(low, mixes[0], mixes[1])
        use = (own * usable_rows(place_ref, 0, WIN, base)) > 0
        before = o_ref[0, base : base + WIN, :].astype(f32)
        o_ref[0, base : base + WIN, :] = jnp.where(use, mix, before).astype(bf16)


def attn_fwd_call(place, q, k, v):
    block = lambda g: pl.BlockSpec((1, S, 2 * HD), lambda p, c: (g ^ c[0], 0, p))
    q, k, v = (a.reshape(CORES, S, DC) for a in (q, k, v))
    return pl.pallas_call(
        attn_fwd_kernel,
        grid_spec=pltpu.PrefetchScalarGridSpec(
            num_scalar_prefetch=1,
            grid=(PAIRS,),
            in_specs=[block(0)] * 3 + [block(1)] * 3,
            out_specs=[
                pl.BlockSpec((CORES, S, 2 * HD), lambda p, c: (0, 0, p)),
                pl.BlockSpec((2, 2, WIN, WIN), lambda p, c: (p, 0, 0, 0)),
                pl.BlockSpec((2, S, S), lambda p, c: (p, 0, 0)),
            ],
        ),
        out_shape=[
            jax.ShapeDtypeStruct((CORES, S, DC), bf16),
            jax.ShapeDtypeStruct((HC, 2, WIN, WIN), bf16),
            jax.ShapeDtypeStruct((HC, S, S), bf16),
        ],
        compiler_params=params(),
        cost_estimate=cost(4 * HC * (S * S + 2 * WIN * WIN) * 128, 12e6, HC * S * S),
    )(place, q, k, v, q, k, v)


def proj_kernel(place_ref, mine_ref, other_ref, x_ref, xo_ref, w0, w1, w2, w3, v_ref, after_ref, h2_ref, w_s):
    @pl.when(pl.program_id(0) == 0)
    def _():
        lay_out(place_ref, (w0, w1, w2, w3), w_s)

    core = place_ref[0]
    at = lambda c: pl.ds(pl.multiple_of(c * DC, DC), DC)
    branch = dot(mine_ref[0], w_s[at(core), :]) + dot(other_ref[0], w_s[at(1 - core), :])
    x = jnp.where(pl.program_id(0) < pl.num_programs(0) // CORES, x_ref[...], xo_ref[...])
    after = x.astype(f32) + (branch + v_ref[7:8, :])
    after_ref[...] = after
    normed, _ = stats(after)
    h2_ref[...] = (normed * v_ref[2:3, :] + v_ref[3:4, :]).astype(bf16)


def proj_call(place, mine, other, x, xo, pieces, vec):
    rows = 288
    half = S // rows
    tile = lambda n: pl.BlockSpec((rows, n), lambda i, c: (i, 0))
    whole = lambda a: pl.BlockSpec(a.shape, lambda i, c: (0,) * a.ndim)
    return pl.pallas_call(
        proj_kernel,
        grid_spec=pltpu.PrefetchScalarGridSpec(
            num_scalar_prefetch=1,
            grid=(T // rows,),
            in_specs=[
                pl.BlockSpec((1, rows, DC), lambda i, c: ((i // half) ^ c[0], i % half, 0)),
                pl.BlockSpec((1, rows, DC), lambda i, c: ((i // half) ^ c[0], i % half, 0)),
                pl.BlockSpec((rows, D), lambda i, c: (jnp.minimum(i, half - 1), 0)),
                pl.BlockSpec((rows, D), lambda i, c: (jnp.maximum(i - half, 0), 0)),
            ]
            + [whole(a) for a in pieces]
            + [whole(vec)],
            out_specs=[tile(D), tile(D)],
            scratch_shapes=[pltpu.VMEM((D, D), bf16)],
        ),
        out_shape=[jax.ShapeDtypeStruct((T, D), f32), jax.ShapeDtypeStruct((T, D), bf16)],
        compiler_params=params(),
        cost_estimate=cost(2 * T * D * D, T * D * 10 + D * D * 2),
    )(place, mine, other, x, xo, *pieces, vec)


K0 = (2.0 / 3.141592653589793) ** 0.5
FT = 768


def gelu_slope(u):
    sq = u * u
    th = jnp.tanh(u * (K0 + (K0 * 0.044715) * sq))
    half = 0.5 + 0.5 * th
    return u * half, half + (u * (half - half * half)) * (2 * K0 + (6 * K0 * 0.044715) * sq)


def mlp_kernel(
    place_ref, h2_ref, gy_ref, w10, w11, w12, w13, w2_ref, b1_ref, mlp_ref, mlpo_ref, gh2b_ref, act_ref, gup_ref, gb1_ref, w1_s
):
    i = pl.program_id(0)

    @pl.when(i == 0)
    def _():
        lay_out(place_ref, (w10, w11, w12, w13), w1_s)
        gb1_ref[...] = jnp.zeros_like(gb1_ref)

    for f in range(FC // FT):
        c = slice(f * FT, (f + 1) * FT)
        act, slope = gelu_slope(dot(h2_ref[...], w1_s[:, c]) + b1_ref[:, c])
        act_ref[:, c] = act.astype(bf16)
        gup = (dot_t(gy_ref[...], w2_ref[c, :]) * slope).astype(bf16)
        gup_ref[:, c] = gup
        gb1_ref[:, c] += jnp.sum(gup.astype(f32), axis=0, keepdims=True)
    gh2b_ref[...] = dot_t(gup_ref[...], w1_s[...]).astype(bf16)
    mlp = dot(act_ref[...], w2_ref[...])
    half = pl.num_programs(0) // CORES

    @pl.when(i < half)
    def _():
        mlp_ref[...] = mlp

    @pl.when(i >= half)
    def _():
        mlpo_ref[...] = mlp


def mlp_call(place, h2, gy, pieces, w2, b1):
    rows = 288
    half = S // rows
    tile = lambda n: pl.BlockSpec((rows, n), lambda i, c: (i, 0))
    whole = lambda a: pl.BlockSpec(a.shape, lambda i, c: (0,) * a.ndim)
    return pl.pallas_call(
        mlp_kernel,
        grid_spec=pltpu.PrefetchScalarGridSpec(
            num_scalar_prefetch=1,
            grid=(T // rows,),
            in_specs=[tile(D), tile(D)]
            + [whole(a) for a in pieces]
            + [whole(w2), whole(b1)],
            out_specs=[
                pl.BlockSpec((rows, D), lambda i, c: (jnp.minimum(i, half - 1), 0)),
                pl.BlockSpec((rows, D), lambda i, c: (jnp.maximum(i - half, 0), 0)),
                tile(D),
                tile(FC),
                tile(FC),
                pl.BlockSpec((1, FC), lambda i, c: (0, 0)),
            ],
            scratch_shapes=[pltpu.VMEM((D, FC), bf16)],
        ),
        out_shape=[
            jax.ShapeDtypeStruct((S, D), f32),
            jax.ShapeDtypeStruct((S, D), f32),
            jax.ShapeDtypeStruct((T, D), bf16),
            jax.ShapeDtypeStruct((T, FC), bf16),
            jax.ShapeDtypeStruct((T, FC), bf16),
            jax.ShapeDtypeStruct((1, FC), f32),
        ],
        compiler_params=params(),
        cost_estimate=cost(8 * T * D * FC, 30e6, T * FC),
    )(place, h2, gy, *pieces, w2, b1)


def by_line(place_ref, value, block, out_ref):
    core = place_ref[0]
    for n in range(PLANE):
        to = jnp.where(core == 0, n, (n % SIDE) * SIDE + n // SIDE)
        out_ref[pl.ds(pl.multiple_of(to * block, block), block), :] = value[n * block : (n + 1) * block, :].astype(bf16)


def fc_grad_kernel(place_ref, h2_ref, gup_ref, act_ref, gy_ref, gw1_ref, gw2_ref):
    by_line(place_ref, t_dot(act_ref[...], gy_ref[...]), SIDE * FR, gw2_ref)
    by_line(place_ref, t_dot(h2_ref[...], gup_ref[...]), BLOCK, gw1_ref)


def fc_grad_call(place, h2, gup, act, gy):
    whole = lambda a: pl.BlockSpec(a.shape, lambda i, c: (0, 0))
    return pl.pallas_call(
        fc_grad_kernel,
        grid_spec=pltpu.PrefetchScalarGridSpec(
            num_scalar_prefetch=1,
            grid=(2,),
            in_specs=[
                whole(h2),
                pl.BlockSpec((T, FC // 2), lambda i, c: (0, i)),
                whole(act),
                pl.BlockSpec((T, DC), lambda i, c: (0, i)),
            ],
            out_specs=[
                pl.BlockSpec((D, FC // 2), lambda i, c: (0, i)),
                pl.BlockSpec((FC, DC), lambda i, c: (0, i)),
            ],
        ),
        out_shape=[jax.ShapeDtypeStruct((D, FC), bf16), jax.ShapeDtypeStruct((FC, D), bf16)],
        compiler_params=params(),
        cost_estimate=cost(4 * T * D * FC, T * (D + FC) * 4 + D * FC * 4),
    )(place, h2, gup, act, gy)


def mid_kernel(place_ref, after_ref, gy_ref, gh2_ref, other_ref, v_ref, ga_ref, gab_ref, sums_ref):
    i = pl.program_id(0)
    normed, inv_std = stats(after_ref[...])
    gh2 = gh2_ref[...].astype(f32) + other_ref[...].astype(f32)
    gy = gy_ref[...].astype(f32)
    ga = gy + norm_back(gh2, normed, inv_std, v_ref[2:3, :])
    gab = ga.astype(bf16)
    gab_ref[...] = gab

    @pl.when(i == 0)
    def _():
        sums_ref[...] = jnp.zeros_like(sums_ref)

    @pl.when(i < pl.num_programs(0) // CORES)
    def _():
        ga_ref[...] = ga
        sums_ref[0:1, :] += jnp.sum(gh2 * normed, axis=0, keepdims=True)
        sums_ref[1:2, :] += jnp.sum(gh2, axis=0, keepdims=True)
        sums_ref[2:3, :] += jnp.sum(gab.astype(f32), axis=0, keepdims=True)
        sums_ref[3:4, :] += jnp.sum(gy, axis=0, keepdims=True)


def mid_call(place, after, gy, gh2, other, vec):
    rows = 288
    half = S // rows
    tile = lambda n: pl.BlockSpec((rows, n), lambda i, c: (i, 0))
    flipped = pl.BlockSpec((rows, D), lambda i, c: ((i + half) % (2 * half), 0))
    whole = lambda a: pl.BlockSpec(a.shape, lambda i, c: (0,) * a.ndim)
    return pl.pallas_call(
        mid_kernel,
        grid_spec=pltpu.PrefetchScalarGridSpec(
            num_scalar_prefetch=1,
            grid=(T // rows,),
            in_specs=[tile(D), tile(D), tile(D), flipped, whole(vec)],
            out_specs=[
                pl.BlockSpec((rows, D), lambda i, c: (jnp.minimum(i, half - 1), 0)),
                tile(D),
                pl.BlockSpec((8, D), lambda i, c: (0, 0)),
            ],
        ),
        out_shape=[
            jax.ShapeDtypeStruct((S, D), f32),
            jax.ShapeDtypeStruct((T, D), bf16),
            jax.ShapeDtypeStruct((8, D), f32),
        ],
        compiler_params=params(),
        cost_estimate=cost(30 * T * D, T * D * 14),
    )(place, after, gy, gh2, other, vec)


def back_head(q_t, k, v, do, do_t, delta, p, mine, head):
    gp = dot_t(jnp.where(mine, do, jnp.zeros_like(do)), v)
    gs = (p.astype(f32) * (gp - delta)).astype(bf16)
    at = slice(head * HD, (head + 1) * HD)
    return dot(gs, k), dot(q_t[at, :], gs), dot(do_t[at, :], p)


def deltas(do, o, low):
    prod = do.astype(f32) * o.astype(f32)
    d0 = jnp.sum(jnp.where(low, prod, 0.0), axis=-1, keepdims=True)
    d1 = jnp.sum(jnp.where(low, 0.0, prod), axis=-1, keepdims=True)
    return d0, d1


def attn_bwd_kernel(
    place_ref,
    q0, k0, v0, o0, p0, cos0, sin0, pos0,
    q1, k1, v1, o1, p1, cos1, sin1, pos1,
    h1t_ref, ga_ref, cols_ref, mine_ref, other_ref, w0, w1, w2, w3, y0, y1, y2, y3,
    gw0, gw1, gw2, gw3, gh_ref, gho_ref, sums_ref,
    gq_s, gk_s, gv_s, gqkv_s, w_s, gw_s, y_s, do_s,
):
    lane = lax.broadcasted_iota(jnp.int32, (1, 2 * HD), 1)
    low = lane < HD
    pair = pl.program_id(0)
    core = place_ref[0]

    @pl.when(pair == 0)
    def _():
        lay_out(place_ref, (y0, y1, y2, y3), y_s)

    wy = y_s[pl.ds(pl.multiple_of(core * DC + pair * 2 * HD, 2 * HD), 2 * HD), :]
    for frame in range(CORES):
        do_s[frame] = dot_t(ga_ref[frame], wy).astype(bf16)

    def finish(frame, q, k, cos_ref, sin_ref, pos_ref):
        cosine, sine = cos_ref[0], sin_ref[0]
        gq = gq_s[...] * HD ** (-0.5)
        gk = gk_s[...]
        sq, sk = swap_halves(gq), swap_halves(gk)
        turn = (q.astype(f32) * HD**0.5) * sq + k.astype(f32) * sk
        gq = (gq * cosine - sq * sine).astype(bf16)
        gk = (gk * cosine - sk * sine).astype(bf16)
        gv = gv_s[...].astype(bf16)
        gqkv_s[frame, :, : 2 * HD] = gq
        gqkv_s[frame, :, 2 * HD : 4 * HD] = gk
        gqkv_s[frame, :, 4 * HD :] = gv
        pos = pos_ref[0]
        col = jnp.sum(turn * pos[:, 1:2], axis=0, keepdims=True)
        row = jnp.sum(turn * pos[:, 0:1], axis=0, keepdims=True)
        bias = [jnp.sum(g.astype(f32), axis=0, keepdims=True) for g in (gq, gk, gv)]
        return jnp.concatenate([col, row] + bias, axis=0)

    q, k, v, do = q1[0], k1[0], v1[0], do_s[1 ^ core]
    d = deltas(do, o1[0], low)
    q_t, do_t = q.astype(f32).T.astype(bf16), do.astype(f32).T.astype(bf16)
    out = [
        back_head(q_t, k, v, do, do_t, d[head], p1[head], mine, head)
        for head, mine in ((0, low), (1, ~low))
    ]
    gq_s[...] = jnp.where(low, out[0][0], out[1][0])
    gk_s[...] = jnp.concatenate([out[0][1], out[1][1]], axis=0).T
    gv_s[...] = jnp.concatenate([out[0][2], out[1][2]], axis=0).T
    sums1 = finish(1, q, k, cos1, sin1, pos1)
    gq_s[...] = jnp.zeros_like(gq_s)
    gk_s[...] = jnp.zeros_like(gk_s)
    gv_s[...] = jnp.zeros_like(gv_s)
    for win, base in enumerate(WINDOWS):
        at = pl.ds(base, WIN)
        q, k, v, o = (r[0, at, :] for r in (q0, k0, v0, o0))
        do = do_s[core, at, :]
        d = deltas(do, o, low)
        q_t, do_t = q.astype(f32).T.astype(bf16), do.astype(f32).T.astype(bf16)
        out = [
            back_head(q_t, k, v, do, do_t, d[head], p0[head, win], mine, head)
            for head, mine in ((0, low), (1, ~low))
        ]
        gq_s[at, :] += jnp.where(low, out[0][0], out[1][0])
        gk_s[at, :] += jnp.concatenate([out[0][1], out[1][1]], axis=0).T
        gv_s[at, :] += jnp.concatenate([out[0][2], out[1][2]], axis=0).T
    sums0 = finish(0, q0[0], k0[0], cos0, sin0, pos0)
    sums_ref[0, 0:5, :] = sums0 + sums1
    sums_ref[0, 5:8, :] = jnp.zeros((3, 2 * HD), f32)

    lay_out(place_ref, (w0, w1, w2, w3), w_s)
    gw = jnp.zeros((D, 6 * HD), f32)
    gw_mine = jnp.zeros((2 * HD, DC), f32)
    gw_other = jnp.zeros((2 * HD, DC), f32)
    for frame, out in ((0, gh_ref), (1, gho_ref)):
        g = gqkv_s[frame ^ core]
        gw += dot(h1t_ref[frame], g)
        gh = dot_t(g, w_s[...])

        @pl.when(pair == 0)
        def _(out=out, gh=gh):
            out[...] = gh

        @pl.when(pair > 0)
        def _(out=out, gh=gh):
            out[...] += gh

        cols = cols_ref[frame].astype(f32).T.astype(bf16)
        gw_mine += dot(cols, mine_ref[frame ^ core])
        gw_other += dot(cols, other_ref[frame ^ core])
    gw_s[:, : 6 * HD] = gw.astype(bf16)
    at = lambda c: pl.ds(pl.multiple_of(c * DC, DC), DC)
    gw_s[at(core), 6 * HD :] = gw_mine.T.astype(bf16)
    gw_s[at(1 - core), 6 * HD :] = gw_other.T.astype(bf16)
    for d, out in enumerate((gw0, gw1, gw2, gw3)):
        a = (place_ref[1] + d) & (SIDE - 1)
        for g in range(SIDE):
            at = pl.multiple_of(natural(core, a, g) * BLOCK, BLOCK)
            out[g * BLOCK : (g + 1) * BLOCK, :] = gw_s[pl.ds(at, BLOCK), :]


def attn_bwd_call(place, q, k, v, ga, mine, other, p0, p1, cosine, sine, pos, h1t, pieces, proj_pieces):
    q, k, v, cosine, sine = (a.reshape(CORES, S, DC) for a in (q, k, v, cosine, sine))
    ga = ga.reshape(CORES, S, D)
    block = lambda g: pl.BlockSpec((1, S, 2 * HD), lambda p, c: (g ^ c[0], 0, p))
    own = lambda g: pl.BlockSpec((1, S, 2 * HD), lambda p, c: (g, 0, p))
    quarter = pl.BlockSpec((QUARTER, 6 * HD), lambda p, c: (0, p))
    grads = pl.BlockSpec((QUARTER, 8 * HD), lambda p, c: (0, p))
    at = lambda g: pl.BlockSpec((1, S, 8), lambda p, c: (g ^ c[0], 0, 0))
    whole = lambda a: pl.BlockSpec(a.shape, lambda p, c: (0,) * a.ndim)
    return pl.pallas_call(
        attn_bwd_kernel,
        grid_spec=pltpu.PrefetchScalarGridSpec(
            num_scalar_prefetch=1,
            grid=(PAIRS,),
            in_specs=[block(0)] * 3
            + [own(0), pl.BlockSpec((2, 2, WIN, WIN), lambda p, c: (p, 0, 0, 0))]
            + [block(0)] * 2
            + [at(0)]
            + [block(1)] * 3
            + [own(1), pl.BlockSpec((2, S, S), lambda p, c: (p, 0, 0))]
            + [block(1)] * 2
            + [at(1)]
            + [whole(h1t), whole(ga), pl.BlockSpec((CORES, S, 2 * HD), lambda p, c: (0, 0, PAIRS * c[0] + p))]
            + [whole(mine), whole(other)]
            + [quarter] * 4
            + [whole(a) for a in proj_pieces],
            out_specs=[grads] * 4
            + [
                pl.BlockSpec((S, D), lambda p, c: (0, 0)),
                pl.BlockSpec((S, D), lambda p, c: (0, 0)),
                pl.BlockSpec((1, 8, 2 * HD), lambda p, c: (p, 0, 0)),
            ],
            scratch_shapes=[pltpu.VMEM((S, 2 * HD), f32)] * 3
            + [pltpu.VMEM((CORES, S, 6 * HD), bf16)]
            + [pltpu.VMEM((D, 6 * HD), bf16), pltpu.VMEM((D, 8 * HD), bf16)]
            + [pltpu.VMEM((D, D), bf16), pltpu.VMEM((CORES, S, 2 * HD), bf16)],
        ),
        out_shape=[
            *[jax.ShapeDtypeStruct((QUARTER, 4 * DC), bf16)] * 4,
            jax.ShapeDtypeStruct((S, D), f32),
            jax.ShapeDtypeStruct((S, D), f32),
            jax.ShapeDtypeStruct((PAIRS, 8, 2 * HD), f32),
        ],
        compiler_params=params(),
        cost_estimate=cost(10 * HC * S * S * 128 + 4 * T * D * 4 * DC, 36e6),
    )(
        place,
        q, k, v, mine, p0, cosine, sine, pos,
        q, k, v, mine, p1, cosine, sine, pos,
        h1t, ga, ga, mine, other, *pieces, *proj_pieces,
    )


def last_kernel(x_ref, ga_ref, gh_ref, other_ref, after_ref, mlp_ref, mlpo_ref, v_ref, gt_ref, out_ref):
    normed, inv_std = stats(x_ref[...].astype(f32))
    gt_ref[...] = ga_ref[...] + norm_back(gh_ref[...] + other_ref[...], normed, inv_std, v_ref[0:1, :])
    out_ref[...] = (after_ref[...] + (mlp_ref[...] + mlpo_ref[...] + v_ref[8:9, :])).astype(bf16)


def last_call(x, ga, gh, other, after, mlp, mlp_other, vec):
    rows = 288
    tile = lambda n: pl.BlockSpec((rows, n), lambda i: (i, 0))
    return pl.pallas_call(
        last_kernel,
        grid=(S // rows,),
        in_specs=[tile(D)] * 7 + [pl.BlockSpec(vec.shape, lambda i: (0, 0))],
        out_specs=[tile(D), tile(D)],
        out_shape=[jax.ShapeDtypeStruct((S, D), f32), jax.ShapeDtypeStruct((S, D), bf16)],
        compiler_params=params(),
        cost_estimate=cost(30 * S * D, S * D * 28),
    )(x, ga, gh, other, after, mlp, mlp_other, vec)


def vec_kernel(place_ref, x_ref, xo_ref, gh_ref, gho_ref, mid_ref, att_ref, gb1_ref, o0, o1, o2, o3, rows_s, full_s):
    core, me = place_ref[0], place_ref[1]
    rows_s[...] = jnp.zeros_like(rows_s)
    for x, gh in ((x_ref, gh_ref), (xo_ref, gho_ref)):
        normed, _ = stats(x[...].astype(f32))
        g = gh[...]
        rows_s[0:1, :] += jnp.sum(g * normed, axis=0, keepdims=True)
        rows_s[1:2, :] += jnp.sum(g, axis=0, keepdims=True)
    rows_s[2:4, :] = mid_ref[0:2, :]
    rows_s[7:9, :] = mid_ref[2:4, :]
    att = jnp.concatenate([att_ref[p] for p in range(PAIRS)], axis=1)
    rows_s[4:7, pl.ds(pl.multiple_of(core * DC, DC), DC)] = att[2:5, :]
    src = lax.broadcasted_iota(jnp.int32, (DC, D), 0)
    dst = lax.broadcasted_iota(jnp.int32, (DC, D), 1)
    want = core * (DC // 2) + (src // HD) * (HD // 2) + (src & (HD // 2 - 1))
    lane = lax.broadcasted_iota(jnp.int32, (1, DC), 1)
    turn = jnp.where((lane & (HD - 1)) < HD // 2, att, -att)
    rows_s[9:10, :] = (
        exact_dot(turn, dst == want)[0:1, :] + exact_dot(turn, dst == want + D // 2)[1:2, :]
    )
    gb1 = jnp.concatenate([gb1_ref[:, r * DC : (r + 1) * DC] for r in range(FC // DC)] * 2, axis=0)
    rows_s[10:14, :] = exact_dot(gb1, spots_t(core))[:4, :]
    full_s[...] = rows_s[...].T
    for d, out in enumerate((o0, o1, o2, o3)):
        a = (me + d) & (SIDE - 1)
        for g in range(SIDE):
            at = pl.multiple_of(natural(core, a, g) * BLOCK, BLOCK)
            out[g * BLOCK : (g + 1) * BLOCK, :] = full_s[pl.ds(at, BLOCK), :]


def vec_call(place, x, xo, gh, gho, mid, att, gb1):
    whole = lambda a: pl.BlockSpec(a.shape, lambda i, c: (0,) * a.ndim)
    return pl.pallas_call(
        vec_kernel,
        grid_spec=pltpu.PrefetchScalarGridSpec(
            num_scalar_prefetch=1,
            grid=(1,),
            in_specs=[whole(a) for a in (x, xo, gh, gho, mid, att, gb1)],
            out_specs=[pl.BlockSpec((QUARTER, 128), lambda i, c: (0, 0))] * 4,
            scratch_shapes=[pltpu.VMEM((128, D), f32), pltpu.VMEM((D, 128), f32)],
        ),
        out_shape=[jax.ShapeDtypeStruct((QUARTER, 128), f32)] * 4,
        compiler_params=params(),
        cost_estimate=cost(20 * T * D, T * D * 6),
    )(place, x, xo, gh, gho, mid, att, gb1)


PACK = 4 * DC + 128 + 2 * FC


def pack_kernel(q0, q1, q2, q3, v0, v1, v2, v3, f1_ref, f2_ref, out_ref):
    qs = q0[...].astype(f32) + q1[...].astype(f32) + q2[...].astype(f32) + q3[...].astype(f32)
    vs = v0[...] + v1[...] + v2[...] + v3[...]
    f1 = f1_ref[...].astype(f32)
    f2 = f2_ref[...].astype(f32)
    for n in range(PLANE):
        at = slice(n * KR, (n + 1) * KR)
        out_ref[n, :, : 4 * DC] = qs[at, :].astype(bf16)
        out_ref[n, :, 4 * DC : 4 * DC + 128] = vs[at, :].astype(bf16)
        out_ref[n, :, 4 * DC + 128 : 4 * DC + 128 + FC] = f1[at, :].astype(bf16)
        for h in range(2):
            to = 4 * DC + 128 + FC + h * D
            out_ref[n, :, to : to + D] = f2[(2 * n + h) * KR : (2 * n + h + 1) * KR, :].astype(bf16)


def pack_call(qs, vs, f1, f2):
    return pl.pallas_call(
        pack_kernel,
        out_shape=jax.ShapeDtypeStruct((PLANE, KR, PACK), bf16),
        compiler_params=params(),
        cost_estimate=cost(QUARTER * PACK * 4, QUARTER * PACK * 8),
    )(*qs, *vs, f1, f2)


def sum_kernel(in_ref, out_ref):
    total = in_ref[0].astype(f32)
    for n in range(1, PLANE):
        total += in_ref[n].astype(f32)
    out_ref[...] = total


def sum_call(packed):
    return pl.pallas_call(
        sum_kernel,
        out_shape=jax.ShapeDtypeStruct((KR, PACK), f32),
        compiler_params=params(),
        cost_estimate=cost(QUARTER * PACK, QUARTER * PACK * 2),
    )(packed)


RATES = (D ** (-0.5), max(1, 2 * D // S) ** (-0.5), D ** (-0.5), FF ** (-0.5), RATE_VECTOR)


def adam_kernel(place_ref, norm_ref, mine_ref, other_ref, *refs):
    masters, firsts, seconds = refs[0:5], refs[5:10], refs[10:15]
    outs = refs[15:30]
    norm_out, bias_out = refs[30:32]
    core = place_ref[0]
    mine, other = mine_ref[...], other_ref[...]
    g0 = jnp.where(core == 0, mine, other)
    g1 = jnp.where(core == 0, other, mine)
    total = jnp.sum(jnp.sum(norm_ref[...], axis=0)[0:1, 0:1], axis=(0, 1), keepdims=True)
    grad_norm = jnp.sqrt(total)
    norm_out[...] = jnp.broadcast_to(grad_norm, norm_out.shape)
    clip = jnp.minimum(1.0, CLIP_LIMIT / (grad_norm + 1e-06))

    def update(i, at, grad):
        clipped = grad * clip
        master = masters[i][at]
        first = BETA_ONE * firsts[i][at] + (1.0 - BETA_ONE) * clipped
        second = BETA_TWO * seconds[i][at] + (1.0 - BETA_TWO) * clipped * clipped
        first_hat = first / (1.0 - BETA_ONE**STEP)
        second_hat = second / (1.0 - BETA_TWO**STEP)
        decay = 0.0 if i == 4 else DECAY_RATE
        outs[3 * i][at] = master - RATES[i] * (first_hat / (jnp.sqrt(second_hat) + ADAM_EPS) + decay * master)
        outs[3 * i + 1][at] = first
        outs[3 * i + 2][at] = second

    rows = slice(None)
    for c, g in ((0, g0), (1, g1)):
        for p in range(PAIRS):
            for i in range(3):
                col = i * D + c * DC + p * 128
                update(0, (rows, slice(col, col + 128)), g[:, (4 * p + i) * 128 : (4 * p + i + 1) * 128])
            col = c * DC + p * 128
            update(1, (rows, slice(col, col + 128)), g[:, (4 * p + 3) * 128 : (4 * p + 4) * 128])
        base = 4 * DC + 128 + FC
        for h in range(2):
            row = c * FR + h * KR
            update(3, (slice(row, row + KR), rows), g[:, base + h * D : base + (h + 1) * D])
    base = 4 * DC + 128
    for r in range(FC // DC):
        at = slice(base + r * DC, base + (r + 1) * DC)
        part = exact_dot(g0[:, at], spots_t(0)) + exact_dot(g1[:, at], spots_t(1))
        update(2, (rows, slice(r * D, (r + 1) * D)), part)
    vec = (g0 + g1)[:, 4 * DC : 4 * DC + 128]
    vec = jnp.concatenate([vec, jnp.zeros((16 - KR, 128), f32)], axis=0).T[:16, :KR]
    update(4, (rows, rows), vec[: masters[4].shape[0], :])
    bias_out[...] = vec[7:8, :] * clip


def adam_call(place, norm, mine, other, masters, firsts, seconds):
    whole = lambda a: pl.BlockSpec(a.shape, lambda i, c: (0,) * len(a.shape))
    args = [norm, mine, other, *masters, *firsts, *seconds]
    shapes = [jax.ShapeDtypeStruct(m.shape, f32) for m in masters for _ in range(3)]
    shapes += [jax.ShapeDtypeStruct((1, 128), f32), jax.ShapeDtypeStruct((1, KR), f32)]
    return pl.pallas_call(
        adam_kernel,
        grid_spec=pltpu.PrefetchScalarGridSpec(
            num_scalar_prefetch=1,
            grid=(1,),
            in_specs=[whole(a) for a in args],
            out_specs=[whole(a) for a in shapes],
        ),
        out_shape=shapes,
        compiler_params=params(),
        cost_estimate=cost(20 * KR * FF * 3, 3e6),
    )(place, *args)


def local(
    tokens,
    cotangent,
    counts,
    patch_row,
    patch_col,
    w_qkv,
    w_proj,
    w_fc1,
    w_fc2,
    vectors,
    m_qkv,
    v_qkv,
    m_proj,
    v_proj,
    m_fc1,
    v_fc1,
    m_fc2,
    v_fc2,
    m_vectors,
    v_vectors,
):
    core = lax.axis_index("grp")
    chip = lax.axis_index("dp")
    first_core = core == 0
    along = jnp.where(first_core, chip // PLANE, (chip // SIDE) % SIDE)
    vr = vectors.shape[0]

    def swap(a):
        return lax.ppermute(a, "grp", [(0, 1), (1, 0)])

    def halves(a):
        n = a.shape[-1] // 2
        return jnp.where(first_core, a[..., :n], a[..., n:])

    def over_plane(share):
        got = plane_swap(jnp.broadcast_to(share[None], (PLANE,) + share.shape))
        return got.reshape(PLANE * share.shape[0], share.shape[1])

    def along_line(quarter):
        return [quarter] + [shift(quarter, d) for d in range(1, SIDE)]

    def line_sum(whole):
        return lax.psum_scatter(whole, BOTH, scatter_dimension=0, axis_index_groups=lines(), tiled=True)

    fc2_b = w_fc2.astype(bf16)
    full_fc2 = lax.all_gather(jnp.where(first_core, fc2_b[:FR], fc2_b[FR:]), "dp", axis=0, tiled=True)
    qkv_b = w_qkv.astype(bf16)
    parts = [halves(qkv_b[:, i * D : (i + 1) * D]) for i in range(3)]
    by_pair = [parts[i][:, p * 128 : (p + 1) * 128] for p in range(PAIRS) for i in range(3)]
    vec_t = jnp.pad(vectors.astype(bf16).T, ((0, 0), (0, 128 - vr)))
    quarter = over_plane(jnp.concatenate(by_pair + [vec_t], axis=1))
    vec_pieces = along_line(quarter[:, 3 * DC :])
    qkv_pieces = along_line(quarter[:, : 3 * DC])
    fc1_b = w_fc1.astype(bf16).reshape(KR, CHIPS, CORES, FR)
    share_fc1 = jnp.where(first_core, fc1_b[:, :, 0], fc1_b[:, :, 1]).reshape(KR, FC)
    share = jnp.concatenate([share_fc1, w_proj.astype(bf16)], axis=1)
    share, vec_pieces = lax.optimization_barrier((share, vec_pieces))
    quarter = over_plane(share)
    proj_pieces = along_line(quarter[:, FC:])
    fc1_pieces = along_line(quarter[:, :FC])

    x_own = tokens.reshape(S, D)
    cot_own = cotangent.reshape(S, D)
    x_other, cot_other = swap(x_own), swap(cot_own)
    ints = jnp.concatenate(
        [
            patch_row.reshape(1, S),
            patch_col.reshape(1, S),
            jnp.pad(counts.reshape(1, 2), ((0, 0), (0, S - 2))),
            jnp.zeros((5, S), jnp.int32),
        ]
    )
    ints = jnp.stack([ints, swap(ints)])
    counts0 = jnp.where(first_core, ints[0, 2, :2], ints[1, 2, :2])
    counts1 = jnp.where(first_core, ints[1, 2, :1], ints[0, 2, :1])
    place = jnp.concatenate([jnp.stack([core, along]).astype(jnp.int32), counts0, counts1])

    vec, h1, h1t, cosine, sine, gy, b1, pos = pre_call(place, x_own, x_other, cot_own, cot_other, ints, vec_pieces)
    q, k, v = qkv_call(place, h1, qkv_pieces, vec, cosine, sine)
    mine, p0, p1 = attn_fwd_call(place, q, k, v)
    other = swap(mine)
    after, h2 = proj_call(place, mine, other, x_own, x_other, proj_pieces, vec)
    mlp, mlp_part, gh2, act, gup, gb1 = mlp_call(place, h2, gy, fc1_pieces, full_fc2, b1)
    mlp_other = swap(mlp_part)
    other_gh2 = swap(gh2)

    gw1, gw2 = fc_grad_call(place, h2, gup, act, gy)
    sum_fc2 = line_sum(gw2)
    sum_fc1 = line_sum(gw1)
    ga, gab, sums_mid = mid_call(place, after, gy, gh2, other_gh2, vec)
    *gw, gh1, gh1_part, sums_att = attn_bwd_call(
        place, q, k, v, gab, mine, other, p0, p1, cosine, sine, pos, h1t, qkv_pieces, proj_pieces
    )
    gh1_other = swap(gh1_part)

    sums_qkv = [gw[0]] + [shift(gw[d], d) for d in range(1, SIDE)]
    vec_parts = vec_call(place, x_own, x_other, gh1, gh1_part, sums_mid, sums_att, gb1)
    sums_vec = [vec_parts[0]] + [shift(vec_parts[d], d) for d in range(1, SIDE)]
    grads = sum_call(plane_swap(pack_call(sums_qkv, sums_vec, sum_fc1, sum_fc2)))
    gt, mixed = last_call(x_own, ga, gh1, gh1_other, after, mlp, mlp_other, vec)

    grads_other = swap(grads)
    is_vec = (jnp.arange(PACK) >= 4 * DC) & (jnp.arange(PACK) < 4 * DC + 128)
    squares = jnp.where(
        is_vec, (grads + grads_other) * (grads + grads_other), grads * grads + grads_other * grads_other
    )
    squares = jnp.sum(squares)
    norms = lax.all_to_all(jnp.full((CHIPS, 8, 128), squares, f32), "dp", 0, 0)
    *updates, grad_norm, bias_proj_grad = adam_call(
        place,
        norms,
        grads,
        grads_other,
        (w_qkv, w_proj, w_fc1, w_fc2, vectors),
        (m_qkv, m_proj, m_fc1, m_fc2, m_vectors),
        (v_qkv, v_proj, v_fc1, v_fc2, v_vectors),
    )
    return (
        mixed.reshape(1, 1, S, D),
        gt.reshape(1, 1, S, D),
        grad_norm[0, 0],
        *updates,
        bias_proj_grad.reshape(KR),
    )


def solution(mesh):
    frame = P("grp", "dp", None, None)
    ints = P("grp", "dp", None)
    rows = P("dp", None)
    cols = P(None, "dp")
    return jax.shard_map(
        local,
        mesh=mesh,
        in_specs=(frame, frame, ints, ints, ints, rows, rows, rows, rows, cols) + (rows,) * 8 + (cols,) * 2,
        out_specs=(frame, frame, P()) + (rows,) * 12 + (cols,) * 3 + (P("dp"),),
        check_vma=False,
    )
```

profile of v0, /device:TPU:0, one launch (start us, length us, event | category | flops | bytes accessed | tf_op | source)
XLA Modules:
  0.0 301.3 jit_solution(1819589761056908490)
XLA Ops:
  7.3 1.0 convert_element_type.21
  9.0 0.9 convert_element_type.19
  11.7 8.3 %all-to-all-start = ((bf16[16,12,1280]{2,1,0:T(8,128)(2,1)}), bf16[16,12,1280]{2,1,0:T(8,128)(2,1)S(1)}, u32[]{:S(2)}, u32[]{:S(2)}) async-start(bf16[16,12,1280]{2,1,0:T(8,128)(2,1)} %broadcast_in_dim.23), calls=%async_computation | async-start | bytes 1310720 | tf_op jit(solution)/shard_map/all_to_all | solution.py:74
  21.4 1.4 fusion
  23.1 8.3 %all-to-all-done = bf16[16,12,1280]{2,1,0:T(8,128)(2,1)S(1)} async-done(((bf16[16,12,1280]{2,1,0:T(8,128)(2,1)}), bf16[16,12,1280]{2,1,0:T(8,128)(2,1)S(1)}, u32[]{:S(2)}, u32[]{:S(2)}) %all-to-all-start) | async-done | bytes 491552 | tf_op jit(solution)/shard_map/all_to_all | solution.py:74
  31.5 1.0 collective-permute-start.3
  32.5 2.7 collective-permute-start.4
  35.2 1.4 collective-permute-start.5
  41.4 2.3 collective-permute-start.8
  43.6 1.1 broadcast_in_dim.24
  44.8 5.0 %all-to-all-start.1 = ((bf16[16,12,2304]{2,1,0:T(8,128)(2,1)}), bf16[16,12,2304]{2,1,0:T(8,128)(2,1)S(1)}, u32[]{:S(2)}, u32[]{:S(2)}) async-start(bf16[16,12,2304]{2,1,0:T(8,128)(2,1)} %broadcast_in_dim.24), calls=%async_computation.1 | async-start | bytes 2359296 | tf_op jit(solution)/shard_map/all_to_all | solution.py:74
  52.3 11.1 %shard_map.339 = (f32[16,768]{1,0:T(8,128)}, bf16[1152,768]{1,0:T(8,128)(2,1)}, bf16[2,768,576]{2,1,0:T(8,128)(2,1)}, f32[1152,384]{1,0:T(8,128)}, f32[1152,384]...) custom-call(s32[5]{0:T(128)} %pad_add_fusion.2.place_ref, ...), custom_call_target="tpu_custom_call" | custom-call | flops 35389440 | bytes 12386304 | tf_op jit(solution)/shard_map/pallas_call | solution.py:250
  64.2 8.1 %shard_map.340 = (bf16[1152,384]{1,0:T(8,128)(2,1)}, bf16[1152,384]{1,0:T(8,128)(2,1)}, bf16[1152,384]{1,0:T(8,128)(2,1)}) custom-call(s32[5]{0:T(128)} %pad_add_fusion.2.place_ref, bf16[1152,768]{1,0:T(8,128)(2,1)} %get-tuple-element.85.h_ref, bf16[192,1152]{1,0:T(8,128)(2,1)} %slice.143.w0, bf16[192,1152]{1,0:T(8,128)(2,1)} %copy-done.13, ...), custom_call_target="tpu_custom_call" | custom-call | flops 2038431744 | bytes 9732096 | tf_op jit(solution)/shard_map/pallas_call | solution.py:306
  72.3 11.3 %shard_map.341 = (bf16[2,576,384]{2,1,0:T(8,128)(2,1)}, bf16[6,2,208,208]{3,2,1,0:T(8,128)(2,1)}, bf16[6,576,576]{2,1,0:T(8,128)(2,1)}) custom-call(s32[5]{0:T(128)} %pad_add_fusion.2.place_ref, bf16[2,576,384]{2,1,0:T(8,128)(2,1)} %bitcast.29, bf16[2,576,384]{2,1,0:T(8,128)(2,1)} %bitcast.33, bf16[2,576,384]{2,1,0:T(8,128)(2,1)} %bitcast.37, ...), custom_call_target="tpu_custom_call" | custom-call | flops 1285029888 | bytes 12000000 | tf_op jit(solution)/shard_map/pallas_call | solution.py:362
  84.6 2.6 collective-permute-start.11
  87.3 1.0 collective-permute-start.13
  88.3 2.6 collective-permute-start.14
  90.9 1.7 collective-permute-done.10.w1.y1
  92.5 1.1 collective-permute-start.15
  93.7 2.2 collective-permute-done.11.w2.y2
  95.9 12.9 %collective-permute-done.12.w3.y3 = bf16[192,768]{1,0:T(8,128)(2,1)S(1)} collective-permute-done((bf16[192,768]{1,0:T(8,128)(2,1)S(1)}, bf16[192,768]{1,0:T(8,128)(2,1)S(1)}, u32[]{:S(2)}, u32[]{:S(2)}) %collective-permute-start.12) | collective-permute-done | bytes 294944 | tf_op jit(solution)/shard_map/ppermute | solution.py:70
  109.5 7.8 %shard_map.342 = (f32[1152,768]{1,0:T(8,128)}, bf16[1152,768]{1,0:T(8,128)(2,1)}) custom-call(s32[5]{0:T(128)} %pad_add_fusion.2.place_ref, bf16[2,576,384]{2,1,0:T(8,128)(2,1)} %get-tuple-element.92.mine_ref.o0.o1, bf16[2,576,384]{2,1,0:T(8,128)(2,1)} %collective-permute-done.9.other_ref, bf16[576,768]{1,0:T(8,128)(2,1)} %bitcast.42, ...), custom_call_target="tpu_custom_call" | custom-call | flops 1358954496 | bytes 10027008 | tf_op jit(solution)/shard_map/pallas_call | solution.py:404
  118.5 18.6 %shard_map.343 = (f32[576,768]{1,0:T(8,128)}, f32[576,768]{1,0:T(8,128)}, bf16[1152,768]{1,0:T(8,128)(2,1)}, bf16[1152,1536]{1,0:T(8,128)(2,1)}, bf16[1152,1536]{1,0:T(8,128)(2,1)}, /*index=5*/f32[1,1536]{1,0:T(1,128)}) custom-call(s32[5]{0:T(128)} %pad_add_fusion.2.place_ref, bf16[1152,768]{1,0:T(8,128)(2,1)} %get-tuple-element.96.h2_ref, ...), custom_call_target="tpu_custom_call" | custom-call | flops 10871635968 | bytes 30000000 | tf_op jit(solution)/shard_map/pallas_call | solution.py:472
  137.2 12.8 %shard_map.348 = (bf16[768,1536]{1,0:T(8,128)(2,1)}, bf16[1536,768]{1,0:T(8,128)(2,1)}) custom-call(s32[5]{0:T(128)} %pad_add_fusion.2.place_ref, bf16[1152,768]{1,0:T(8,128)(2,1)} %get-tuple-element.96.h2_ref, bf16[1152,1536]{1,0:T(8,128)(2,1)} %get-tuple-element.122.gup_ref, bf16[1152,1536]{1,0:T(8,128)(2,1)} %get-tuple-element.123.act_ref, ...), custom_call_target="tpu_custom_call" | custom-call | flops 5435817984 | bytes 15335424 | tf_op jit(solution)/shard_map/pallas_call | solution.py:517
  151.8 3.6 %collective-permute-done.16.other_ref = bf16[1152,768]{1,0:T(8,128)(2,1)S(1)} collective-permute-done((bf16[1152,768]{1,0:T(8,128)(2,1)S(1)}, bf16[1152,768]{1,0:T(8,128)(2,1)S(1)}, u32[]{:S(2)}, u32[]{:S(2)}) %collective-permute-start.16) | collective-permute-done | bytes 1769504 | tf_op jit(solution)/shard_map/ppermute | solution.py:966
  155.4 1.2 copy-done.4
  156.6 8.1 %shard_map.344 = (f32[576,768]{1,0:T(8,128)}, bf16[1152,768]{1,0:T(8,128)(2,1)}, f32[8,768]{1,0:T(8,128)}) custom-call(s32[5]{0:T(128)} %pad_add_fusion.2.place_ref, f32[1152,768]{1,0:T(8,128)} %get-tuple-element.94.after_ref, bf16[1152,768]{1,0:T(8,128)(2,1)} %get-tuple-element.95.gy_ref, bf16[1152,768]{1,0:T(8,128)(2,1)} %get-tuple-element.98.gh2_ref, ...), custom_call_target="tpu_custom_call" | custom-call | flops 26542080 | bytes 12386304 | tf_op jit(solution)/shard_map/pallas_call | solution.py:567
  164.7 29.0 %shard_map.345 = (bf16[192,1536]{1,0:T(8,128)(2,1)}, bf16[192,1536]{1,0:T(8,128)(2,1)}, bf16[192,1536]{1,0:T(8,128)(2,1)}, bf16[192,1536]{1,0:T(8,128)(2,1)}, f3...) custom-call(s32[5]{0:T(128)} %pad_add_fusion.2.place_ref, bf16[2,576,384]{2,1,0:T(8,128)(2,1)} %bitcast.31, ...), custom_call_target="tpu_custom_call" | custom-call | flops 7983857664 | bytes 36000000 | tf_op jit(solution)/shard_map/pallas_call | solution.py:713
  193.7 1.8 collective-permute-start.19
  195.5 2.3 collective-permute-start.20
  197.8 1.2 collective-permute-start.21
  198.9 6.3 %shard_map.347 = (f32[192,128]{1,0:T(8,128)}, f32[192,128]{1,0:T(8,128)}, f32[192,128]{1,0:T(8,128)}, f32[192,128]{1,0:T(8,128)}) custom-call(s32[5]{0:T(128)} %pad_add_fusion.2.place_ref, bf16[576,768]{1,0:T(8,128)(2,1)} %bitcast.43, bf16[576,768]{1,0:T(8,128)(2,1)} %copy-done.2, f32[576,768]{1,0:T(8,128)} %get-tuple-element.105.gh_ref, ...), custom_call_target="tpu_custom_call" | custom-call | flops 17694720 | bytes 5308416 | tf_op jit(solution)/shard_map/pallas_call | solution.py:809
  205.3 0.9 collective-permute-start.22
  206.2 1.3 collective-permute-start.23
  207.5 9.2 %collective-permute-done.22.v1 = f32[192,128]{1,0:T(8,128)S(1)} collective-permute-done((f32[192,128]{1,0:T(8,128)}, f32[192,128]{1,0:T(8,128)S(1)}, u32[]{:S(2)}, u32[]{:S(2)}) %collective-permute-start.22) | collective-permute-done | bytes 98336 | tf_op jit(solution)/shard_map/ppermute | solution.py:70
  216.9 4.8 %collective-permute-done.24.v3 = f32[192,128]{1,0:T(8,128)S(1)} collective-permute-done((f32[192,128]{1,0:T(8,128)}, f32[192,128]{1,0:T(8,128)S(1)}, u32[]{:S(2)}, u32[]{:S(2)}) %collective-permute-start.24) | collective-permute-done | bytes 98336 | tf_op jit(solution)/shard_map/ppermute | solution.py:70
  222.9 3.9 %shard_map.349 = bf16[16,12,4736]{2,1,0:T(8,128)(2,1)} custom-call(bf16[192,1536]{1,0:T(8,128)(2,1)} %get-tuple-element.111.q0, bf16[192,1536]{1,0:T(8,128)(2,1)} %copy-done.9, bf16[192,1536]{1,0:T(8,128)(2,1)} %copy-done.10, bf16[192,1536]{1,0:T(8,128)(2,1)} %copy-done.11, f32[192,128]{1,0:T(8,128)} %get-tuple-element.118.v0, f32[192,128]{1,0:T(8,128)} %copy-done.19, ...), custom_call_target="tpu_custom_call" | custom-call | flops 3637248 | bytes 7274496 | tf_op jit(solution)/shard_map/pallas_call | solution.py:843
  226.8 7.2 %all-to-all-start.2 = ((bf16[16,12,4736]{2,1,0:T(8,128)(2,1)}), bf16[16,12,4736]{2,1,0:T(8,128)(2,1)S(1)}, u32[]{:S(2)}, u32[]{:S(2)}) async-start(bf16[16,12,4736]{2,1,0:T(8,128)(2,1)} %shard_map.349), calls=%async_computation.4 | async-start | bytes 4849664 | tf_op jit(solution)/shard_map/all_to_all | solution.py:74
  234.7 26.5 %all-to-all-done.2.in_ref = bf16[16,12,4736]{2,1,0:T(8,128)(2,1)S(1)} async-done(((bf16[16,12,4736]{2,1,0:T(8,128)(2,1)}), bf16[16,12,4736]{2,1,0:T(8,128)(2,1)S(1)}, u32[]{:S(2)}, u32[]{:S(2)}) %all-to-all-start.2) | async-done | bytes 1818656 | tf_op jit(solution)/shard_map/all_to_all | solution.py:74
  261.2 1.4 copy-done
  262.6 2.7 shard_map.350.mine_ref
  265.3 1.8 collective-permute-done.25.other_ref
  267.1 1.8 select_reduce_fusion
  268.9 1.4 broadcast_in_dim.26
  270.2 7.2 %all-to-all-start.3 = ((f32[64,8,128]{2,1,0:T(8,128)}), f32[64,8,128]{2,1,0:T(8,128)S(1)}, u32[]{:S(2)}, u32[]{:S(2)}) async-start(f32[64,8,128]{2,1,0:T(8,128)} %broadcast_in_dim.26), calls=%async_computation.5 | async-start | bytes 524288 | tf_op jit(solution)/shard_map/all_to_all | solution.py:1045
  277.4 6.0 %shard_map.346 = (f32[576,768]{1,0:T(8,128)}, bf16[576,768]{1,0:T(8,128)(2,1)}) custom-call(bf16[576,768]{1,0:T(8,128)(2,1)} %bitcast.44, f32[576,768]{1,0:T(8,128)} %get-tuple-element.99.ga_ref, f32[576,768]{1,0:T(8,128)} %get-tuple-element.105.gh_ref, f32[576,768]{1,0:T(8,128)} %collective-permute-done.17.other_ref, ...), custom_call_target="tpu_custom_call" | custom-call | flops 13271040 | bytes 12386304 | tf_op jit(solution)/shard_map/pallas_call | solution.py:766
  283.4 4.7 %all-to-all-done.3.norm_ref = f32[64,8,128]{2,1,0:T(8,128)S(1)} async-done(((f32[64,8,128]{2,1,0:T(8,128)}), f32[64,8,128]{2,1,0:T(8,128)S(1)}, u32[]{:S(2)}, u32[]{:S(2)}) %all-to-all-start.3) | async-done | bytes 262176 | tf_op jit(solution)/shard_map/all_to_all | solution.py:1045
  288.9 5.7 %shard_map.351 = (f32[12,2304]{1,0:T(8,128)}, f32[12,2304]{1,0:T(8,128)}, f32[12,2304]{1,0:T(8,128)}, f32[12,768]{1,0:T(8,128)}, f32[12,768]{1,0:T(8,128)}, /*in...) custom-call(s32[5]{0:T(128)} %pad_add_fusion.2.place_ref, ...), custom_call_target="tpu_custom_call" | custom-call | flops 2211840 | bytes 3000000 | tf_op jit(solution)/shard_map/pallas_call | solution.py:923
  (136 shorter events, 18.1 us)
Async XLA Ops:
  7.2 12.8 %copy-start.26 = (s32[1,1,576]{2,1,0:T(1,128)S(1)}, s32[1,1,576]{2,1,0:T(1,128)}, u32[]{:S(2)}) copy-start(s32[1,1,576]{2,1,0:T(1,128)} %param.23) | copy-start | bytes 6916
  7.2 12.8 %copy-start.25 = (s32[1,1,576]{2,1,0:T(1,128)S(1)}, s32[1,1,576]{2,1,0:T(1,128)}, u32[]{:S(2)}) copy-start(s32[1,1,576]{2,1,0:T(1,128)} %param.24) | copy-start | bytes 6916
  7.2 12.8 %copy-start.27 = (s32[1,1,2]{2,1,0:T(1,128)S(1)}, s32[1,1,2]{2,1,0:T(1,128)}, u32[]{:S(2)}) copy-start(s32[1,1,2]{2,1,0:T(1,128)} %param.22) | copy-start | bytes 28
  7.2 12.9 %copy-start.1 = (bf16[1,1,576,768]{3,2,1,0:T(8,128)(2,1)S(1)}, bf16[1,1,576,768]{3,2,1,0:T(8,128)(2,1)}, u32[]{:S(2)}) copy-start(bf16[1,1,576,768]{3,2,1,0:T(8,128)(2,1)} %param.20) | copy-start | bytes 2654212
  7.2 13.5 %copy-start.8 = (f32[12,3072]{1,0:T(8,128)S(1)}, f32[12,3072]{1,0:T(8,128)}, u32[]{:S(2)}) copy-start(f32[12,3072]{1,0:T(8,128)} %refs_2_.1) | copy-start | bytes 442372
  7.2 110.2 %all-gather.2.cloned.1.call-start = ((), (), s32[]{:S(2)}) async-start(), calls=%async_computation.6 | async-start | bytes 2396160 | tf_op jit(solution)/shard_map/all_gather | solution.py:983
  11.7 11.4 %copy-start.18 = (f32[12,768]{1,0:T(8,128)S(1)}, f32[12,768]{1,0:T(8,128)}, u32[]{:S(2)}) copy-start(f32[12,768]{1,0:T(8,128)} %refs_1_.1) | copy-start | bytes 110596
  11.7 19.7 %all-to-all-start = ((bf16[16,12,1280]{2,1,0:T(8,128)(2,1)}), bf16[16,12,1280]{2,1,0:T(8,128)(2,1)S(1)}, u32[]{:S(2)}, u32[]{:S(2)}) async-start(bf16[16,12,1280]{2,1,0:T(8,128)(2,1)} %broadcast_in_dim.23), calls=%async_computation | async-start | bytes 1310720 | tf_op jit(solution)/shard_map/all_to_all | solution.py:74
  20.1 15.1 %collective-permute-start = (s32[8,576]{1,0:T(8,128)S(1)}, s32[8,576]{1,0:T(8,128)S(1)}, u32[]{:S(2)}, u32[]{:S(2)}) collective-permute-start(s32[8,576]{1,0:T(8,128)S(1)} %get-tuple-element.147), channel_id=1, source_target_pairs={{0,64},{64,0},{1,65},{65,1},{2,66},{66,2},{3,67},{67,3},{4,68},{68... | collective-permute-start | bytes 55304 | tf_op jit(solution)/shard_map/ppermute | solution.py:966
  20.2 31.2 %collective-permute-start.1 = (bf16[576,768]{1,0:T(8,128)(2,1)S(1)}, bf16[576,768]{1,0:T(8,128)(2,1)S(1)}, u32[]{:S(2)}, u32[]{:S(2)}) collective-permute-start(bf16[576,768]{1,0:T(8,128)(2,1)S(1)} %bitcast.45), channel_id=1, source_target_pairs={{0,64},{64,0},{1,65},{65,1},{2,66},{66,2},{3,67},{67,3},{4,68},{68... | collective-permute-start | bytes 2654216 | tf_op jit(solution)/shard_map/ppermute | solution.py:966
  20.7 30.7 %collective-permute-start.2 = (bf16[576,768]{1,0:T(8,128)(2,1)}, bf16[576,768]{1,0:T(8,128)(2,1)}, u32[]{:S(2)}, u32[]{:S(2)}) collective-permute-start(bf16[576,768]{1,0:T(8,128)(2,1)} %bitcast.52), channel_id=1, source_target_pairs={{0,64},{64,0},{1,65},{65,1},{2,66},{66,2},{3,67},{67,3},{4,68},{68... | collective-permute-start | bytes 2654216 | tf_op jit(solution)/shard_map/ppermute | solution.py:966
  31.5 13.2 %copy-start.17 = (bf16[192,128]{1,0:T(8,128)(2,1)}, bf16[192,128]{1,0:T(8,128)(2,1)S(1)}, u32[]{:S(2)}) copy-start(bf16[192,128]{1,0:T(8,128)(2,1)S(1)} %slice.142.v0) | copy-start | bytes 147460
  31.5 8.3 %collective-permute-start.3 = (bf16[192,128]{1,0:T(8,128)(2,1)S(1)}, bf16[192,128]{1,0:T(8,128)(2,1)S(1)}, u32[]{:S(2)}, u32[]{:S(2)}) collective-permute-start(bf16[192,128]{1,0:T(8,128)(2,1)S(1)} %slice.142.v0), channel_id=1, source_target_pairs={{0,16},{16,32},{32,48},{48,0},{1,17},{17,33},{33,49},{49,1},{2,18}... | collective-permute-start | bytes 147464 | tf_op jit(solution)/shard_map/ppermute | solution.py:70
  32.5 8.0 %collective-permute-start.4 = (bf16[192,128]{1,0:T(8,128)(2,1)S(1)}, bf16[192,128]{1,0:T(8,128)(2,1)S(1)}, u32[]{:S(2)}, u32[]{:S(2)}) collective-permute-start(bf16[192,128]{1,0:T(8,128)(2,1)S(1)} %slice.142.v0), channel_id=1, source_target_pairs={{0,32},{16,48},{32,0},{48,16},{1,33},{17,49},{33,1},{49,17},{2,34}... | collective-permute-start | bytes 147464 | tf_op jit(solution)/shard_map/ppermute | solution.py:70
  35.2 6.1 %collective-permute-start.5 = (bf16[192,128]{1,0:T(8,128)(2,1)S(1)}, bf16[192,128]{1,0:T(8,128)(2,1)S(1)}, u32[]{:S(2)}, u32[]{:S(2)}) collective-permute-start(bf16[192,128]{1,0:T(8,128)(2,1)S(1)} %slice.142.v0), channel_id=1, source_target_pairs={{0,48},{16,0},{32,16},{48,32},{1,49},{17,1},{33,17},{49,33},{2,50}... | collective-permute-start | bytes 147464 | tf_op jit(solution)/shard_map/ppermute | solution.py:70
  39.9 4.9 %copy-start.22 = (bf16[192,128]{1,0:T(8,128)(2,1)}, bf16[192,128]{1,0:T(8,128)(2,1)S(1)}, u32[]{:S(2)}) copy-start(bf16[192,128]{1,0:T(8,128)(2,1)S(1)} %collective-permute-done.3.v1) | copy-start | bytes 147460
  39.9 23.5 %collective-permute-start.6 = (bf16[192,1152]{1,0:T(8,128)(2,1)}, bf16[192,1152]{1,0:T(8,128)(2,1)S(1)}, u32[]{:S(2)}, u32[]{:S(2)}) collective-permute-start(bf16[192,1152]{1,0:T(8,128)(2,1)} %slice.143.w0), channel_id=1, source_target_pairs={{0,16},{16,32},{32,48},{48,0},{1,17},{17,33},{33,49},{49,1},{2,18}... | collective-permute-start | bytes 1327112 | tf_op jit(solution)/shard_map/ppermute | solution.py:70
  40.5 23.0 %collective-permute-start.7 = (bf16[192,1152]{1,0:T(8,128)(2,1)}, bf16[192,1152]{1,0:T(8,128)(2,1)}, u32[]{:S(2)}, u32[]{:S(2)}) collective-permute-start(bf16[192,1152]{1,0:T(8,128)(2,1)} %slice.143.w0), channel_id=1, source_target_pairs={{0,32},{16,48},{32,0},{48,16},{1,33},{17,49},{33,1},{49,17},{2,34}... | collective-permute-start | bytes 1327112 | tf_op jit(solution)/shard_map/ppermute | solution.py:70
  41.4 22.1 %collective-permute-start.8 = (bf16[192,1152]{1,0:T(8,128)(2,1)}, bf16[192,1152]{1,0:T(8,128)(2,1)}, u32[]{:S(2)}, u32[]{:S(2)}) collective-permute-start(bf16[192,1152]{1,0:T(8,128)(2,1)} %slice.143.w0), channel_id=1, source_target_pairs={{0,48},{16,0},{32,16},{48,32},{1,49},{17,1},{33,17},{49,33},{2,50}... | collective-permute-start | bytes 1327112 | tf_op jit(solution)/shard_map/ppermute | solution.py:70
  44.8 39.0 %all-to-all-start.1 = ((bf16[16,12,2304]{2,1,0:T(8,128)(2,1)}), bf16[16,12,2304]{2,1,0:T(8,128)(2,1)S(1)}, u32[]{:S(2)}, u32[]{:S(2)}) async-start(bf16[16,12,2304]{2,1,0:T(8,128)(2,1)} %broadcast_in_dim.24), calls=%async_computation.1 | async-start | bytes 2359296 | tf_op jit(solution)/shard_map/all_to_all | solution.py:74
  49.8 172.0 %reduce-scatter.3.cloned.1.call-start = ((), (), s32[]{:S(2)}) async-start(), calls=%async_computation.7 | async-start | bytes 2949120 | tf_op jit(solution)/shard_map/reduce_scatter | solution.py:980
  83.7 25.2 %collective-permute-start.9 = (bf16[2,576,384]{2,1,0:T(8,128)(2,1)}, bf16[2,576,384]{2,1,0:T(8,128)(2,1)}, u32[]{:S(2)}, u32[]{:S(2)}) collective-permute-start(bf16[2,576,384]{2,1,0:T(8,128)(2,1)} %get-tuple-element.92.mine_ref.o0.o1), channel_id=1, source_target_pairs={{0,64},{64,0},{1,65},{65,1},{2,66},{66,2},{3,67},{67,3},{4,68},{68... | collective-permute-start | bytes 2654216 | tf_op jit(solution)/shard_map/ppermute | solution.py:966
  84.0 24.8 %copy-start.6 = (bf16[192,768]{1,0:T(8,128)(2,1)}, bf16[192,768]{1,0:T(8,128)(2,1)S(1)}, u32[]{:S(2)}) copy-start(bf16[192,768]{1,0:T(8,128)(2,1)S(1)} %slice.144.w0.y0) | copy-start | bytes 884740
  84.0 8.5 %collective-permute-start.10 = (bf16[192,768]{1,0:T(8,128)(2,1)S(1)}, bf16[192,768]{1,0:T(8,128)(2,1)S(1)}, u32[]{:S(2)}, u32[]{:S(2)}) collective-permute-start(bf16[192,768]{1,0:T(8,128)(2,1)S(1)} %slice.144.w0.y0), channel_id=1, source_target_pairs={{0,16},{16,32},{32,48},{48,0},{1,17},{17,33},{33,49},{49,1},{2,18}... | collective-permute-start | bytes 884744 | tf_op jit(solution)/shard_map/ppermute | solution.py:70
  84.6 11.3 %collective-permute-start.11 = (bf16[192,768]{1,0:T(8,128)(2,1)S(1)}, bf16[192,768]{1,0:T(8,128)(2,1)S(1)}, u32[]{:S(2)}, u32[]{:S(2)}) collective-permute-start(bf16[192,768]{1,0:T(8,128)(2,1)S(1)} %slice.144.w0.y0), channel_id=1, source_target_pairs={{0,32},{16,48},{32,0},{48,16},{1,33},{17,49},{33,1},{49,17},{2,34}... | collective-permute-start | bytes 884744 | tf_op jit(solution)/shard_map/ppermute | solution.py:70
  87.3 30.1 %copy-start.12 = (bf16[192,1536]{1,0:T(8,128)(2,1)}, bf16[192,1536]{1,0:T(8,128)(2,1)S(1)}, u32[]{:S(2)}) copy-start(bf16[192,1536]{1,0:T(8,128)(2,1)S(1)} %slice.145.w10) | copy-start | bytes 1769476
  87.3 30.1 %collective-permute-start.13 = (bf16[192,1536]{1,0:T(8,128)(2,1)S(1)}, bf16[192,1536]{1,0:T(8,128)(2,1)S(1)}, u32[]{:S(2)}, u32[]{:S(2)}) collective-permute-start(bf16[192,1536]{1,0:T(8,128)(2,1)S(1)} %slice.145.w10), channel_id=1, source_target_pairs={{0,16},{16,32},{32,48},{48,0},{1,17},{17,33},{33,49},{49,1},{2,18}... | collective-permute-start | bytes 1769480 | tf_op jit(solution)/shard_map/ppermute | solution.py:70
  88.3 29.1 %collective-permute-start.14 = (bf16[192,1536]{1,0:T(8,128)(2,1)S(1)}, bf16[192,1536]{1,0:T(8,128)(2,1)S(1)}, u32[]{:S(2)}, u32[]{:S(2)}) collective-permute-start(bf16[192,1536]{1,0:T(8,128)(2,1)S(1)} %slice.145.w10), channel_id=1, source_target_pairs={{0,32},{16,48},{32,0},{48,16},{1,33},{17,49},{33,1},{49,17},{2,34}... | collective-permute-start | bytes 1769480 | tf_op jit(solution)/shard_map/ppermute | solution.py:70
  92.5 16.3 %copy-start.14 = (bf16[192,768]{1,0:T(8,128)(2,1)}, bf16[192,768]{1,0:T(8,128)(2,1)S(1)}, u32[]{:S(2)}) copy-start(bf16[192,768]{1,0:T(8,128)(2,1)S(1)} %collective-permute-done.10.w1.y1) | copy-start | bytes 884740
  92.5 24.8 %collective-permute-start.15 = (bf16[192,1536]{1,0:T(8,128)(2,1)S(1)}, bf16[192,1536]{1,0:T(8,128)(2,1)S(1)}, u32[]{:S(2)}, u32[]{:S(2)}) collective-permute-start(bf16[192,1536]{1,0:T(8,128)(2,1)S(1)} %slice.145.w10), channel_id=1, source_target_pairs={{0,48},{16,0},{32,16},{48,32},{1,49},{17,1},{33,17},{49,33},{2,50}... | collective-permute-start | bytes 1769480 | tf_op jit(solution)/shard_map/ppermute | solution.py:70
  95.9 13.0 %copy-start.15 = (bf16[192,768]{1,0:T(8,128)(2,1)}, bf16[192,768]{1,0:T(8,128)(2,1)S(1)}, u32[]{:S(2)}) copy-start(bf16[192,768]{1,0:T(8,128)(2,1)S(1)} %collective-permute-done.11.w2.y2) | copy-start | bytes 884740
  95.9 12.9 %collective-permute-start.12 = (bf16[192,768]{1,0:T(8,128)(2,1)S(1)}, bf16[192,768]{1,0:T(8,128)(2,1)S(1)}, u32[]{:S(2)}, u32[]{:S(2)}) collective-permute-start(bf16[192,768]{1,0:T(8,128)(2,1)S(1)} %slice.144.w0.y0), channel_id=1, source_target_pairs={{0,48},{16,0},{32,16},{48,32},{1,49},{17,1},{33,17},{49,33},{2,50}... | collective-permute-start | bytes 884744 | tf_op jit(solution)/shard_map/ppermute | solution.py:70
  150.0 71.7 %reduce-scatter.5.cloned.1.call-start = ((), (), s32[]{:S(2)}) async-start(), calls=%async_computation.8 | async-start | bytes 2949120 | tf_op jit(solution)/shard_map/reduce_scatter | solution.py:980
  151.5 3.8 %collective-permute-start.16 = (bf16[1152,768]{1,0:T(8,128)(2,1)S(1)}, bf16[1152,768]{1,0:T(8,128)(2,1)S(1)}, u32[]{:S(2)}, u32[]{:S(2)}) collective-permute-start(bf16[1152,768]{1,0:T(8,128)(2,1)S(1)} %copy-done.3), channel_id=1, source_target_pairs={{0,64},{64,0},{1,65},{65,1},{2,66},{66,2},{3,67},{67,3},{4,68},{68... | collective-permute-start | bytes 5308424 | tf_op jit(solution)/shard_map/ppermute | solution.py:966
  193.7 28.0 %collective-permute-start.19 = (bf16[192,1536]{1,0:T(8,128)(2,1)}, bf16[192,1536]{1,0:T(8,128)(2,1)S(1)}, u32[]{:S(2)}, u32[]{:S(2)}) collective-permute-start(bf16[192,1536]{1,0:T(8,128)(2,1)} %get-tuple-element.112), channel_id=1, source_target_pairs={{0,16},{16,32},{32,48},{48,0},{1,17},{17,33},{33,49},{49,1},{2,18}... | collective-permute-start | bytes 1769480 | tf_op jit(solution)/shard_map/ppermute | solution.py:70
  195.5 26.2 %collective-permute-start.20 = (bf16[192,1536]{1,0:T(8,128)(2,1)}, bf16[192,1536]{1,0:T(8,128)(2,1)S(1)}, u32[]{:S(2)}, u32[]{:S(2)}) collective-permute-start(bf16[192,1536]{1,0:T(8,128)(2,1)} %get-tuple-element.113), channel_id=1, source_target_pairs={{0,32},{16,48},{32,0},{48,16},{1,33},{17,49},{33,1},{49,17},{2,34}... | collective-permute-start | bytes 1769480 | tf_op jit(solution)/shard_map/ppermute | solution.py:70
  197.8 23.9 %collective-permute-start.21 = (bf16[192,1536]{1,0:T(8,128)(2,1)}, bf16[192,1536]{1,0:T(8,128)(2,1)S(1)}, u32[]{:S(2)}, u32[]{:S(2)}) collective-permute-start(bf16[192,1536]{1,0:T(8,128)(2,1)} %get-tuple-element.114), channel_id=1, source_target_pairs={{0,48},{16,0},{32,16},{48,32},{1,49},{17,1},{33,17},{49,33},{2,50}... | collective-permute-start | bytes 1769480 | tf_op jit(solution)/shard_map/ppermute | solution.py:70
  205.3 11.4 %collective-permute-start.22 = (f32[192,128]{1,0:T(8,128)}, f32[192,128]{1,0:T(8,128)S(1)}, u32[]{:S(2)}, u32[]{:S(2)}) collective-permute-start(f32[192,128]{1,0:T(8,128)} %get-tuple-element.119), channel_id=1, source_target_pairs={{0,16},{16,32},{32,48},{48,0},{1,17},{17,33},{33,49},{49,1},{2,18}... | collective-permute-start | bytes 294920 | tf_op jit(solution)/shard_map/ppermute | solution.py:70
  206.2 10.7 %collective-permute-start.23 = (f32[192,128]{1,0:T(8,128)}, f32[192,128]{1,0:T(8,128)S(1)}, u32[]{:S(2)}, u32[]{:S(2)}) collective-permute-start(f32[192,128]{1,0:T(8,128)} %get-tuple-element.120), channel_id=1, source_target_pairs={{0,32},{16,48},{32,0},{48,16},{1,33},{17,49},{33,1},{49,17},{2,34}... | collective-permute-start | bytes 294920 | tf_op jit(solution)/shard_map/ppermute | solution.py:70
  216.7 5.1 %copy-start.19 = (f32[192,128]{1,0:T(8,128)}, f32[192,128]{1,0:T(8,128)S(1)}, u32[]{:S(2)}) copy-start(f32[192,128]{1,0:T(8,128)S(1)} %collective-permute-done.22.v1) | copy-start | bytes 294916
  216.7 5.0 %collective-permute-start.24 = (f32[192,128]{1,0:T(8,128)}, f32[192,128]{1,0:T(8,128)S(1)}, u32[]{:S(2)}, u32[]{:S(2)}) collective-permute-start(f32[192,128]{1,0:T(8,128)} %get-tuple-element.121), channel_id=1, source_target_pairs={{0,48},{16,0},{32,16},{48,32},{1,49},{17,1},{33,17},{49,33},{2,50}... | collective-permute-start | bytes 294920 | tf_op jit(solution)/shard_map/ppermute | solution.py:70
  216.9 4.9 %copy-start.20 = (f32[192,128]{1,0:T(8,128)}, f32[192,128]{1,0:T(8,128)S(1)}, u32[]{:S(2)}) copy-start(f32[192,128]{1,0:T(8,128)S(1)} %collective-permute-done.23.v2) | copy-start | bytes 294916
  226.8 34.3 %all-to-all-start.2 = ((bf16[16,12,4736]{2,1,0:T(8,128)(2,1)}), bf16[16,12,4736]{2,1,0:T(8,128)(2,1)S(1)}, u32[]{:S(2)}, u32[]{:S(2)}) async-start(bf16[16,12,4736]{2,1,0:T(8,128)(2,1)} %shard_map.349), calls=%async_computation.4 | async-start | bytes 4849664 | tf_op jit(solution)/shard_map/all_to_all | solution.py:74
  234.1 43.4 %collective-permute-start.18 = (f32[576,768]{1,0:T(8,128)}, f32[576,768]{1,0:T(8,128)}, u32[]{:S(2)}, u32[]{:S(2)}) collective-permute-start(f32[576,768]{1,0:T(8,128)} %get-tuple-element.108), channel_id=1, source_target_pairs={{0,64},{64,0},{1,65},{65,1},{2,66},{66,2},{3,67},{67,3},{4,68},{68... | collective-permute-start | bytes 5308424 | tf_op jit(solution)/shard_map/ppermute | solution.py:966
  234.2 43.3 %collective-permute-start.17 = (f32[576,768]{1,0:T(8,128)}, f32[576,768]{1,0:T(8,128)}, u32[]{:S(2)}, u32[]{:S(2)}) collective-permute-start(f32[576,768]{1,0:T(8,128)} %get-tuple-element.106.gho_ref), channel_id=1, source_target_pairs={{0,64},{64,0},{1,65},{65,1},{2,66},{66,2},{3,67},{67,3},{4,68},{68... | collective-permute-start | bytes 5308424 | tf_op jit(solution)/shard_map/ppermute | solution.py:966
  265.3 1.8 collective-permute-start.25
  267.1 16.3 %copy-start.5 = (f32[12,4736]{1,0:T(8,128)}, f32[12,4736]{1,0:T(8,128)S(1)}, u32[]{:S(2)}) copy-start(f32[12,4736]{1,0:T(8,128)S(1)} %collective-permute-done.25.other_ref) | copy-start | bytes 681988
  270.2 17.9 %all-to-all-start.3 = ((f32[64,8,128]{2,1,0:T(8,128)}), f32[64,8,128]{2,1,0:T(8,128)S(1)}, u32[]{:S(2)}, u32[]{:S(2)}) async-start(f32[64,8,128]{2,1,0:T(8,128)} %broadcast_in_dim.26), calls=%async_computation.5 | async-start | bytes 524288 | tf_op jit(solution)/shard_map/all_to_all | solution.py:1045
  (16 other events, 21.6 us)
Sparse Core Ops, SparseCore 0:
  11.5 79.6 all-gather.1
  150.2 26.1 reduce-scatter.2
  178.7 27.7 reduce-scatter.4
where the time goes:
time: 307 us; the launch traced here: 301 us
  Pallas kernels  132 us (43%)
  waiting for transfers between devices  76.5 us (25%)
  starting transfers between devices  54 us (18%)
  local copies, waits for them, and re-layouts  16.1 us (5%)
  between operations  15.9 us (5%)
  other arithmetic  7.16 us (2%)
    all_to_all x3, waiting for transfers between devices, plane_swap(): return lax.all_to_all(value, BOTH, 0, 0, axis_index_groups=planes())  34.8 us
    ppermute x18, waiting for transfers between devices, shift(): return lax.ppermute(value, BOTH, pairs)  30.8 us
    pallas_call x1, Pallas kernels, attn_bwd_call(): pl.pallas_call(attn_bwd_kernel, grid_spec=pltpu.PrefetchScalarGridSpec(nu...  29 us
    ppermute x18, starting transfers between devices, shift(): return lax.ppermute(value, BOTH, pairs)  24.4 us
    all_to_all x3, starting transfers between devices, plane_swap(): return lax.all_to_all(value, BOTH, 0, 0, axis_index_groups=planes())  20.5 us
    pallas_call x1, Pallas kernels, mlp_call(): pl.pallas_call(mlp_kernel, grid_spec=pltpu.PrefetchScalarGridSpec(num_sca...  18.6 us
    pallas_call x1, Pallas kernels, fc_grad_call(): pl.pallas_call(fc_grad_kernel, grid_spec=pltpu.PrefetchScalarGridSpec(num...  12.8 us
    pallas_call x1, Pallas kernels, attn_fwd_call(): pl.pallas_call(attn_fwd_kernel, grid_spec=pltpu.PrefetchScalarGridSpec(nu...  11.3 us
  transfers between devices with their start and end apart: 33, of which 10 were waited for; matrix products, arithmetic and copies ran while one was open for 4% of the time, Pallas kernels for 30%

commit v1 on v0

--- a/solution.py
+++ b/solution.py
@@ -196,8 +196,8 @@
 
 
 def pre_kernel(
-    place_ref, x_ref, xo_ref, c_ref, co_ref, ints_ref, v0, v1, v2, v3,
-    vec_ref, h_ref, ht_ref, cos_ref, sin_ref, gy_ref, b1_ref, pos_ref,
+    place_ref, x_ref, xo_ref, ints_ref, v0, v1, v2, v3,
+    vec_ref, h_ref, ht_ref, cos_ref, sin_ref, b1_ref, pos_ref,
     full_s, rows_s,
 ):
     i = pl.program_id(0)
@@ -217,8 +217,6 @@
     h = normed * rows_s[0:1, :] + rows_s[1:2, :]
     h_ref[...] = h.astype(bf16)
     ht_ref[0] = h.T.astype(bf16)
-    keep = usable_rows(place_ref, i ^ core, S)
-    gy_ref[...] = (jnp.where(mine, c_ref[...], co_ref[...]).astype(f32) * keep).astype(bf16)
     src = lax.broadcasted_iota(jnp.int32, (D, DC), 0)
     dst = lax.broadcasted_iota(jnp.int32, (D, DC), 1)
     want = core * (DC // 2) + (dst // HD) * (HD // 2) + (dst & (HD // 2 - 1))
@@ -244,7 +242,29 @@
         sin_ref[...] = jnp.sin(angle) * sign
 
 
-def pre_call(place, x, xo, c, co, ints, pieces):
+def gy_kernel(place_ref, c_ref, co_ref, gy_ref):
+    i = pl.program_id(0)
+    keep = usable_rows(place_ref, i ^ place_ref[0], S)
+    gy_ref[...] = (jnp.where(i == 0, c_ref[...], co_ref[...]).astype(f32) * keep).astype(bf16)
+
+
+def gy_call(place, c, co):
+    whole = pl.BlockSpec((S, D), lambda i, c: (0, 0))
+    return pl.pallas_call(
+        gy_kernel,
+        grid_spec=pltpu.PrefetchScalarGridSpec(
+            num_scalar_prefetch=1,
+            grid=(CORES,),
+            in_specs=[whole, whole],
+            out_specs=pl.BlockSpec((S, D), lambda i, c: (i, 0)),
+        ),
+        out_shape=jax.ShapeDtypeStruct((T, D), bf16),
+        compiler_params=params(),
+        cost_estimate=cost(4 * T * D, T * D * 4),
+    )(place, c, co)
+
+
+def pre_call(place, x, xo, ints, pieces):
     tile = lambda n: pl.BlockSpec((S, n), lambda i, c: (i, 0))
     whole = lambda a: pl.BlockSpec(a.shape, lambda i, c: (0,) * a.ndim)
     return pl.pallas_call(
@@ -252,7 +272,7 @@
         grid_spec=pltpu.PrefetchScalarGridSpec(
             num_scalar_prefetch=1,
             grid=(CORES,),
-            in_specs=[whole(a) for a in (x, xo, c, co)]
+            in_specs=[whole(a) for a in (x, xo)]
             + [pl.BlockSpec((1, 8, S), lambda i, c: (i, 0, 0))]
             + [whole(a) for a in pieces],
             out_specs=[
@@ -261,7 +281,6 @@
                 pl.BlockSpec((1, D, S), lambda i, c: (i, 0, 0)),
                 tile(DC),
                 tile(DC),
-                tile(D),
                 pl.BlockSpec((1, FC), lambda i, c: (0, 0)),
                 pl.BlockSpec((1, S, 8), lambda i, c: (i, 0, 0)),
             ],
@@ -273,13 +292,12 @@
             jax.ShapeDtypeStruct((CORES, D, S), bf16),
             jax.ShapeDtypeStruct((T, DC), f32),
             jax.ShapeDtypeStruct((T, DC), f32),
-            jax.ShapeDtypeStruct((T, D), bf16),
             jax.ShapeDtypeStruct((1, FC), f32),
             jax.ShapeDtypeStruct((CORES, S, 8), f32),
         ],
         compiler_params=params(),
         cost_estimate=cost(T * (20 * D + 40 * DC), T * (D * 10 + DC * 8)),
-    )(place, x, xo, c, co, ints, *pieces)
+    )(place, x, xo, ints, *pieces)
 
 
 def qkv_kernel(place_ref, h_ref, w0, w1, w2, w3, v_ref, cos_ref, sin_ref, q_out, k_out, v_out, w_s):
@@ -423,6 +441,7 @@
     )(place, mine, other, x, xo, *pieces, vec)
 
 
+PACK = 4 * DC + 128
 K0 = (2.0 / 3.141592653589793) ** 0.5
 FT = 768
 
@@ -435,23 +454,19 @@
 
 
 def mlp_kernel(
-    place_ref, h2_ref, gy_ref, w10, w11, w12, w13, w2_ref, b1_ref, mlp_ref, mlpo_ref, gh2b_ref, act_ref, gup_ref, gb1_ref, w1_s
+    place_ref, h2_ref, w10, w11, w12, w13, w2_ref, b1_ref, mlp_ref, mlpo_ref, act_ref, slope_ref, w1_s
 ):
     i = pl.program_id(0)
 
     @pl.when(i == 0)
     def _():
         lay_out(place_ref, (w10, w11, w12, w13), w1_s)
-        gb1_ref[...] = jnp.zeros_like(gb1_ref)
 
     for f in range(FC // FT):
         c = slice(f * FT, (f + 1) * FT)
         act, slope = gelu_slope(dot(h2_ref[...], w1_s[:, c]) + b1_ref[:, c])
         act_ref[:, c] = act.astype(bf16)
-        gup = (dot_t(gy_ref[...], w2_ref[c, :]) * slope).astype(bf16)
-        gup_ref[:, c] = gup
-        gb1_ref[:, c] += jnp.sum(gup.astype(f32), axis=0, keepdims=True)
-    gh2b_ref[...] = dot_t(gup_ref[...], w1_s[...]).astype(bf16)
+        slope_ref[:, c] = slope.astype(bf16)
     mlp = dot(act_ref[...], w2_ref[...])
     half = pl.num_programs(0) // CORES
 
@@ -464,7 +479,7 @@
         mlpo_ref[...] = mlp
 
 
-def mlp_call(place, h2, gy, pieces, w2, b1):
+def mlp_call(place, h2, pieces, w2, b1):
     rows = 288
     half = S // rows
     tile = lambda n: pl.BlockSpec((rows, n), lambda i, c: (i, 0))
@@ -474,30 +489,61 @@
         grid_spec=pltpu.PrefetchScalarGridSpec(
             num_scalar_prefetch=1,
             grid=(T // rows,),
-            in_specs=[tile(D), tile(D)]
-            + [whole(a) for a in pieces]
-            + [whole(w2), whole(b1)],
+            in_specs=[tile(D)] + [whole(a) for a in pieces] + [whole(w2), whole(b1)],
             out_specs=[
                 pl.BlockSpec((rows, D), lambda i, c: (jnp.minimum(i, half - 1), 0)),
                 pl.BlockSpec((rows, D), lambda i, c: (jnp.maximum(i - half, 0), 0)),
-                tile(D),
                 tile(FC),
                 tile(FC),
-                pl.BlockSpec((1, FC), lambda i, c: (0, 0)),
             ],
             scratch_shapes=[pltpu.VMEM((D, FC), bf16)],
         ),
         out_shape=[
             jax.ShapeDtypeStruct((S, D), f32),
             jax.ShapeDtypeStruct((S, D), f32),
+            jax.ShapeDtypeStruct((T, FC), bf16),
+            jax.ShapeDtypeStruct((T, FC), bf16),
+        ],
+        compiler_params=params(),
+        cost_estimate=cost(4 * T * D * FC, 20e6, T * FC),
+    )(place, h2, *pieces, w2, b1)
+
+
+def mlp_back_kernel(place_ref, gy_ref, slope_ref, w10, w11, w12, w13, w2_ref, gh2_ref, gup_ref, gb1_ref, w1_s):
+    @pl.when(pl.program_id(0) == 0)
+    def _():
+        lay_out(place_ref, (w10, w11, w12, w13), w1_s)
+        gb1_ref[...] = jnp.zeros_like(gb1_ref)
+
+    for f in range(FC // FT):
+        c = slice(f * FT, (f + 1) * FT)
+        gup = (dot_t(gy_ref[...], w2_ref[c, :]) * slope_ref[:, c].astype(f32)).astype(bf16)
+        gup_ref[:, c] = gup
+        gb1_ref[:, c] += jnp.sum(gup.astype(f32), axis=0, keepdims=True)
+    gh2_ref[...] = dot_t(gup_ref[...], w1_s[...]).astype(bf16)
+
+
+def mlp_back_call(place, gy, slope, pieces, w2):
+    rows = 288
+    tile = lambda n: pl.BlockSpec((rows, n), lambda i, c: (i, 0))
+    whole = lambda a: pl.BlockSpec(a.shape, lambda i, c: (0,) * a.ndim)
+    return pl.pallas_call(
+        mlp_back_kernel,
+        grid_spec=pltpu.PrefetchScalarGridSpec(
+            num_scalar_prefetch=1,
+            grid=(T // rows,),
+            in_specs=[tile(D), tile(FC)] + [whole(a) for a in pieces] + [whole(w2)],
+            out_specs=[tile(D), tile(FC), pl.BlockSpec((1, FC), lambda i, c: (0, 0))],
+            scratch_shapes=[pltpu.VMEM((D, FC), bf16)],
+        ),
+        out_shape=[
             jax.ShapeDtypeStruct((T, D), bf16),
-            jax.ShapeDtypeStruct((T, FC), bf16),
             jax.ShapeDtypeStruct((T, FC), bf16),
             jax.ShapeDtypeStruct((1, FC), f32),
         ],
         compiler_params=params(),
-        cost_estimate=cost(8 * T * D * FC, 30e6, T * FC),
-    )(place, h2, gy, *pieces, w2, b1)
+        cost_estimate=cost(4 * T * D * FC, 16e6),
+    )(place, gy, slope, *pieces, w2)
 
 
 def by_line(place_ref, value, block, out_ref):
@@ -507,33 +553,42 @@
         out_ref[pl.ds(pl.multiple_of(to * block, block), block), :] = value[n * block : (n + 1) * block, :].astype(bf16)
 
 
-def fc_grad_kernel(place_ref, h2_ref, gup_ref, act_ref, gy_ref, gw1_ref, gw2_ref):
-    by_line(place_ref, t_dot(act_ref[...], gy_ref[...]), SIDE * FR, gw2_ref)
-    by_line(place_ref, t_dot(h2_ref[...], gup_ref[...]), BLOCK, gw1_ref)
-
-
-def fc_grad_call(place, h2, gup, act, gy):
-    whole = lambda a: pl.BlockSpec(a.shape, lambda i, c: (0, 0))
-    return pl.pallas_call(
-        fc_grad_kernel,
-        grid_spec=pltpu.PrefetchScalarGridSpec(
-            num_scalar_prefetch=1,
-            grid=(2,),
-            in_specs=[
-                whole(h2),
-                pl.BlockSpec((T, FC // 2), lambda i, c: (0, i)),
-                whole(act),
-                pl.BlockSpec((T, DC), lambda i, c: (0, i)),
-            ],
-            out_specs=[
-                pl.BlockSpec((D, FC // 2), lambda i, c: (0, i)),
-                pl.BlockSpec((FC, DC), lambda i, c: (0, i)),
-            ],
-        ),
-        out_shape=[jax.ShapeDtypeStruct((D, FC), bf16), jax.ShapeDtypeStruct((FC, D), bf16)],
-        compiler_params=params(),
-        cost_estimate=cost(4 * T * D * FC, T * (D + FC) * 4 + D * FC * 4),
-    )(place, h2, gup, act, gy)
+def fc1_grad_kernel(place_ref, h2_ref, gup_ref, out_ref):
+    by_line(place_ref, t_dot(h2_ref[...], gup_ref[...]), BLOCK, out_ref)
+
+
+def fc1_grad_call(place, h2, gup):
+    return pl.pallas_call(
+        fc1_grad_kernel,
+        grid_spec=pltpu.PrefetchScalarGridSpec(
+            num_scalar_prefetch=1,
+            grid=(FC // FT,),
+            in_specs=[pl.BlockSpec((T, D), lambda i, c: (0, 0)), pl.BlockSpec((T, FT), lambda i, c: (0, i))],
+            out_specs=pl.BlockSpec((D, FT), lambda i, c: (0, i)),
+        ),
+        out_shape=jax.ShapeDtypeStruct((D, FC), bf16),
+        compiler_params=params(),
+        cost_estimate=cost(2 * T * D * FC, T * (D + FC) * 2 + D * FC * 2),
+    )(place, h2, gup)
+
+
+def fc2_grad_kernel(place_ref, act_ref, gy_ref, out_ref):
+    by_line(place_ref, t_dot(act_ref[...], gy_ref[...]), SIDE * FR, out_ref)
+
+
+def fc2_grad_call(place, act, gy):
+    return pl.pallas_call(
+        fc2_grad_kernel,
+        grid_spec=pltpu.PrefetchScalarGridSpec(
+            num_scalar_prefetch=1,
+            grid=(D // DC,),
+            in_specs=[pl.BlockSpec((T, FC), lambda i, c: (0, 0)), pl.BlockSpec((T, DC), lambda i, c: (0, i))],
+            out_specs=pl.BlockSpec((FC, DC), lambda i, c: (0, i)),
+        ),
+        out_shape=jax.ShapeDtypeStruct((FC, D), bf16),
+        compiler_params=params(),
+        cost_estimate=cost(2 * T * D * FC, T * (D + FC) * 2 + D * FC * 2),
+    )(place, act, gy)
 
 
 def mid_kernel(place_ref, after_ref, gy_ref, gh2_ref, other_ref, v_ref, ga_ref, gab_ref, sums_ref):
@@ -600,13 +655,38 @@
     return d0, d1
 
 
+def vec_sums(place_ref, x_ref, xo_ref, gh_ref, gho_ref, mid_ref, att_ref, gb1_ref, rows_s):
+    core = place_ref[0]
+    rows_s[...] = jnp.zeros_like(rows_s)
+    for x, gh in ((x_ref, gh_ref), (xo_ref, gho_ref)):
+        normed, _ = stats(x[...].astype(f32))
+        g = gh[...]
+        rows_s[0:1, :] += jnp.sum(g * normed, axis=0, keepdims=True)
+        rows_s[1:2, :] += jnp.sum(g, axis=0, keepdims=True)
+    rows_s[2:4, :] = mid_ref[0:2, :]
+    rows_s[7:9, :] = mid_ref[2:4, :]
+    att = jnp.concatenate([att_ref[p] for p in range(PAIRS)], axis=1)
+    rows_s[4:7, pl.ds(pl.multiple_of(core * DC, DC), DC)] = att[2:5, :]
+    src = lax.broadcasted_iota(jnp.int32, (DC, D), 0)
+    dst = lax.broadcasted_iota(jnp.int32, (DC, D), 1)
+    want = core * (DC // 2) + (src // HD) * (HD // 2) + (src & (HD // 2 - 1))
+    lane = lax.broadcasted_iota(jnp.int32, (1, DC), 1)
+    turn = jnp.where((lane & (HD - 1)) < HD // 2, att, -att)
+    rows_s[9:10, :] = (
+        exact_dot(turn, dst == want)[0:1, :] + exact_dot(turn, dst == want + D // 2)[1:2, :]
+    )
+    gb1 = jnp.concatenate([gb1_ref[:, r * DC : (r + 1) * DC] for r in range(FC // DC)] * 2, axis=0)
+    rows_s[10:14, :] = exact_dot(gb1, spots_t(core))[:4, :]
+
+
 def attn_bwd_kernel(
     place_ref,
     q0, k0, v0, o0, p0, cos0, sin0, pos0,
     q1, k1, v1, o1, p1, cos1, sin1, pos1,
     h1t_ref, ga_ref, cols_ref, mine_ref, other_ref, w0, w1, w2, w3, y0, y1, y2, y3,
-    gw0, gw1, gw2, gw3, gh_ref, gho_ref, sums_ref,
-    gq_s, gk_s, gv_s, gqkv_s, w_s, gw_s, y_s, do_s,
+    x_ref, xo_ref, mid_ref, gb1_ref,
+    gw0, gw1, gw2, gw3, gh_ref, gho_ref,
+    gq_s, gk_s, gv_s, gqkv_s, w_s, gw_s, y_s, do_s, att_s, rows_s, full_s,
 ):
     lane = lax.broadcasted_iota(jnp.int32, (1, 2 * HD), 1)
     low = lane < HD
@@ -667,8 +747,7 @@
         gk_s[at, :] += jnp.concatenate([out[0][1], out[1][1]], axis=0).T
         gv_s[at, :] += jnp.concatenate([out[0][2], out[1][2]], axis=0).T
     sums0 = finish(0, q0[0], k0[0], cos0, sin0, pos0)
-    sums_ref[0, 0:5, :] = sums0 + sums1
-    sums_ref[0, 5:8, :] = jnp.zeros((3, 2 * HD), f32)
+    att_s[pair, 0:5, :] = sums0 + sums1
 
     lay_out(place_ref, (w0, w1, w2, w3), w_s)
     gw = jnp.zeros((D, 6 * HD), f32)
@@ -694,20 +773,33 @@
     at = lambda c: pl.ds(pl.multiple_of(c * DC, DC), DC)
     gw_s[at(core), 6 * HD :] = gw_mine.T.astype(bf16)
     gw_s[at(1 - core), 6 * HD :] = gw_other.T.astype(bf16)
+    to = pl.ds(pl.multiple_of(pair * 8 * HD, 8 * HD), 8 * HD)
     for d, out in enumerate((gw0, gw1, gw2, gw3)):
         a = (place_ref[1] + d) & (SIDE - 1)
         for g in range(SIDE):
             at = pl.multiple_of(natural(core, a, g) * BLOCK, BLOCK)
-            out[g * BLOCK : (g + 1) * BLOCK, :] = gw_s[pl.ds(at, BLOCK), :]
-
-
-def attn_bwd_call(place, q, k, v, ga, mine, other, p0, p1, cosine, sine, pos, h1t, pieces, proj_pieces):
+            out[g * BLOCK : (g + 1) * BLOCK, to] = gw_s[pl.ds(at, BLOCK), :]
+
+    @pl.when(pair == PAIRS - 1)
+    def _():
+        vec_sums(place_ref, x_ref, xo_ref, gh_ref, gho_ref, mid_ref, att_s, gb1_ref, rows_s)
+        full_s[...] = rows_s[...].T.astype(bf16)
+        for d, out in enumerate((gw0, gw1, gw2, gw3)):
+            a = (place_ref[1] + d) & (SIDE - 1)
+            for g in range(SIDE):
+                at = pl.multiple_of(natural(core, a, g) * BLOCK, BLOCK)
+                out[g * BLOCK : (g + 1) * BLOCK, 4 * DC :] = full_s[pl.ds(at, BLOCK), :]
+
+
+def attn_bwd_call(
+    place, q, k, v, ga, mine, other, p0, p1, cosine, sine, pos, h1t, pieces, proj_pieces, x, xo, mid, gb1
+):
     q, k, v, cosine, sine = (a.reshape(CORES, S, DC) for a in (q, k, v, cosine, sine))
     ga = ga.reshape(CORES, S, D)
     block = lambda g: pl.BlockSpec((1, S, 2 * HD), lambda p, c: (g ^ c[0], 0, p))
     own = lambda g: pl.BlockSpec((1, S, 2 * HD), lambda p, c: (g, 0, p))
     quarter = pl.BlockSpec((QUARTER, 6 * HD), lambda p, c: (0, p))
-    grads = pl.BlockSpec((QUARTER, 8 * HD), lambda p, c: (0, p))
+    keep = lambda *n: pl.BlockSpec(n, lambda p, c: (0,) * len(n))
     at = lambda g: pl.BlockSpec((1, S, 8), lambda p, c: (g ^ c[0], 0, 0))
     whole = lambda a: pl.BlockSpec(a.shape, lambda p, c: (0,) * a.ndim)
     return pl.pallas_call(
@@ -726,23 +818,19 @@
             + [whole(h1t), whole(ga), pl.BlockSpec((CORES, S, 2 * HD), lambda p, c: (0, 0, PAIRS * c[0] + p))]
             + [whole(mine), whole(other)]
             + [quarter] * 4
-            + [whole(a) for a in proj_pieces],
-            out_specs=[grads] * 4
-            + [
-                pl.BlockSpec((S, D), lambda p, c: (0, 0)),
-                pl.BlockSpec((S, D), lambda p, c: (0, 0)),
-                pl.BlockSpec((1, 8, 2 * HD), lambda p, c: (p, 0, 0)),
-            ],
+            + [whole(a) for a in proj_pieces]
+            + [whole(a) for a in (x, xo, mid, gb1)],
+            out_specs=[keep(QUARTER, PACK)] * 4 + [keep(S, D)] * 2,
             scratch_shapes=[pltpu.VMEM((S, 2 * HD), f32)] * 3
             + [pltpu.VMEM((CORES, S, 6 * HD), bf16)]
             + [pltpu.VMEM((D, 6 * HD), bf16), pltpu.VMEM((D, 8 * HD), bf16)]
-            + [pltpu.VMEM((D, D), bf16), pltpu.VMEM((CORES, S, 2 * HD), bf16)],
+            + [pltpu.VMEM((D, D), bf16), pltpu.VMEM((CORES, S, 2 * HD), bf16)]
+            + [pltpu.VMEM((PAIRS, 8, 2 * HD), f32), pltpu.VMEM((128, D), f32), pltpu.VMEM((D, 128), bf16)],
         ),
         out_shape=[
-            *[jax.ShapeDtypeStruct((QUARTER, 4 * DC), bf16)] * 4,
+            *[jax.ShapeDtypeStruct((QUARTER, PACK), bf16)] * 4,
             jax.ShapeDtypeStruct((S, D), f32),
             jax.ShapeDtypeStruct((S, D), f32),
-            jax.ShapeDtypeStruct((PAIRS, 8, 2 * HD), f32),
         ],
         compiler_params=params(),
         cost_estimate=cost(10 * HC * S * S * 128 + 4 * T * D * 4 * DC, 36e6),
@@ -750,7 +838,7 @@
         place,
         q, k, v, mine, p0, cosine, sine, pos,
         q, k, v, mine, p1, cosine, sine, pos,
-        h1t, ga, ga, mine, other, *pieces, *proj_pieces,
+        h1t, ga, ga, mine, other, *pieces, *proj_pieces, x, xo, mid, gb1,
     )
 
 
@@ -774,78 +862,19 @@
     )(x, ga, gh, other, after, mlp, mlp_other, vec)
 
 
-def vec_kernel(place_ref, x_ref, xo_ref, gh_ref, gho_ref, mid_ref, att_ref, gb1_ref, o0, o1, o2, o3, rows_s, full_s):
-    core, me = place_ref[0], place_ref[1]
-    rows_s[...] = jnp.zeros_like(rows_s)
-    for x, gh in ((x_ref, gh_ref), (xo_ref, gho_ref)):
-        normed, _ = stats(x[...].astype(f32))
-        g = gh[...]
-        rows_s[0:1, :] += jnp.sum(g * normed, axis=0, keepdims=True)
-        rows_s[1:2, :] += jnp.sum(g, axis=0, keepdims=True)
-    rows_s[2:4, :] = mid_ref[0:2, :]
-    rows_s[7:9, :] = mid_ref[2:4, :]
-    att = jnp.concatenate([att_ref[p] for p in range(PAIRS)], axis=1)
-    rows_s[4:7, pl.ds(pl.multiple_of(core * DC, DC), DC)] = att[2:5, :]
-    src = lax.broadcasted_iota(jnp.int32, (DC, D), 0)
-    dst = lax.broadcasted_iota(jnp.int32, (DC, D), 1)
-    want = core * (DC // 2) + (src // HD) * (HD // 2) + (src & (HD // 2 - 1))
-    lane = lax.broadcasted_iota(jnp.int32, (1, DC), 1)
-    turn = jnp.where((lane & (HD - 1)) < HD // 2, att, -att)
-    rows_s[9:10, :] = (
-        exact_dot(turn, dst == want)[0:1, :] + exact_dot(turn, dst == want + D // 2)[1:2, :]
-    )
-    gb1 = jnp.concatenate([gb1_ref[:, r * DC : (r + 1) * DC] for r in range(FC // DC)] * 2, axis=0)
-    rows_s[10:14, :] = exact_dot(gb1, spots_t(core))[:4, :]
-    full_s[...] = rows_s[...].T
-    for d, out in enumerate((o0, o1, o2, o3)):
-        a = (me + d) & (SIDE - 1)
-        for g in range(SIDE):
-            at = pl.multiple_of(natural(core, a, g) * BLOCK, BLOCK)
-            out[g * BLOCK : (g + 1) * BLOCK, :] = full_s[pl.ds(at, BLOCK), :]
-
-
-def vec_call(place, x, xo, gh, gho, mid, att, gb1):
-    whole = lambda a: pl.BlockSpec(a.shape, lambda i, c: (0,) * a.ndim)
-    return pl.pallas_call(
-        vec_kernel,
-        grid_spec=pltpu.PrefetchScalarGridSpec(
-            num_scalar_prefetch=1,
-            grid=(1,),
-            in_specs=[whole(a) for a in (x, xo, gh, gho, mid, att, gb1)],
-            out_specs=[pl.BlockSpec((QUARTER, 128), lambda i, c: (0, 0))] * 4,
-            scratch_shapes=[pltpu.VMEM((128, D), f32), pltpu.VMEM((D, 128), f32)],
-        ),
-        out_shape=[jax.ShapeDtypeStruct((QUARTER, 128), f32)] * 4,
-        compiler_params=params(),
-        cost_estimate=cost(20 * T * D, T * D * 6),
-    )(place, x, xo, gh, gho, mid, att, gb1)
-
-
-PACK = 4 * DC + 128 + 2 * FC
-
-
-def pack_kernel(q0, q1, q2, q3, v0, v1, v2, v3, f1_ref, f2_ref, out_ref):
-    qs = q0[...].astype(f32) + q1[...].astype(f32) + q2[...].astype(f32) + q3[...].astype(f32)
-    vs = v0[...] + v1[...] + v2[...] + v3[...]
-    f1 = f1_ref[...].astype(f32)
-    f2 = f2_ref[...].astype(f32)
+def pack_kernel(q0, q1, q2, q3, out_ref):
+    total = q0[...].astype(f32) + q1[...].astype(f32) + q2[...].astype(f32) + q3[...].astype(f32)
     for n in range(PLANE):
-        at = slice(n * KR, (n + 1) * KR)
-        out_ref[n, :, : 4 * DC] = qs[at, :].astype(bf16)
-        out_ref[n, :, 4 * DC : 4 * DC + 128] = vs[at, :].astype(bf16)
-        out_ref[n, :, 4 * DC + 128 : 4 * DC + 128 + FC] = f1[at, :].astype(bf16)
-        for h in range(2):
-            to = 4 * DC + 128 + FC + h * D
-            out_ref[n, :, to : to + D] = f2[(2 * n + h) * KR : (2 * n + h + 1) * KR, :].astype(bf16)
-
-
-def pack_call(qs, vs, f1, f2):
+        out_ref[n] = total[n * KR : (n + 1) * KR, :].astype(bf16)
+
+
+def pack_call(parts):
     return pl.pallas_call(
         pack_kernel,
         out_shape=jax.ShapeDtypeStruct((PLANE, KR, PACK), bf16),
         compiler_params=params(),
-        cost_estimate=cost(QUARTER * PACK * 4, QUARTER * PACK * 8),
-    )(*qs, *vs, f1, f2)
+        cost_estimate=cost(QUARTER * PACK * 4, QUARTER * PACK * 10),
+    )(*parts)
 
 
 def sum_kernel(in_ref, out_ref):
@@ -858,16 +887,66 @@
 def sum_call(packed):
     return pl.pallas_call(
         sum_kernel,
-        out_shape=jax.ShapeDtypeStruct((KR, PACK), f32),
-        compiler_params=params(),
-        cost_estimate=cost(QUARTER * PACK, QUARTER * PACK * 2),
+        out_shape=jax.ShapeDtypeStruct(packed.shape[1:], f32),
+        compiler_params=params(),
+        cost_estimate=cost(packed.size, packed.size * 2),
     )(packed)
 
 
+def fc_kernel(place_ref, f1_ref, f1o_ref, f2_ref, f2o_ref, g1_ref, g2_ref, sq_ref):
+    first = place_ref[0] == 0
+    a, b = f1_ref[...], f1o_ref[...]
+    a, b = jnp.where(first, a, b), jnp.where(first, b, a)
+    for r in range(FC // DC):
+        at = slice(r * DC, (r + 1) * DC)
+        g1_ref[:, r * D : (r + 1) * D] = exact_dot(a[:, at], spots_t(0)) + exact_dot(b[:, at], spots_t(1))
+    c, d = f2_ref[...], f2o_ref[...]
+    g2_ref[:FR, :] = jnp.where(first, c, d)
+    g2_ref[FR:, :] = jnp.where(first, d, c)
+    total = jnp.sum(a * a + b * b, axis=(0, 1), keepdims=True) + jnp.sum(c * c + d * d, axis=(0, 1), keepdims=True)
+    sq_ref[...] = jnp.broadcast_to(total, sq_ref.shape)
+
+
+def fc_call(place, f1, f1o, f2, f2o):
+    whole = lambda a: pl.BlockSpec(a.shape, lambda i, c: (0,) * len(a.shape))
+    args = (f1, f1o, f2, f2o)
+    shapes = [jax.ShapeDtypeStruct(s, f32) for s in ((KR, FF), (2 * FR, D), (8, 128))]
+    return pl.pallas_call(
+        fc_kernel,
+        grid_spec=pltpu.PrefetchScalarGridSpec(
+            num_scalar_prefetch=1,
+            grid=(1,),
+            in_specs=[whole(a) for a in args],
+            out_specs=[whole(a) for a in shapes],
+        ),
+        out_shape=shapes,
+        compiler_params=params(),
+        cost_estimate=cost(6 * KR * DC * D * 8, 1e6),
+    )(place, *args)
+
+
+def norm_kernel(g_ref, o_ref, sq_ref, out_ref):
+    g, o = g_ref[...], o_ref[...]
+    cut = 4 * DC
+    part = jnp.sum(g[:, :cut] * g[:, :cut] + o[:, :cut] * o[:, :cut], axis=(0, 1), keepdims=True)
+    both = g[:, cut:] + o[:, cut:]
+    part += jnp.sum(both * both, axis=(0, 1), keepdims=True)
+    out_ref[...] = jnp.broadcast_to((part + sq_ref[0:1, 0:1])[None], out_ref.shape)
+
+
+def norm_call(g, o, squares):
+    return pl.pallas_call(
+        norm_kernel,
+        out_shape=jax.ShapeDtypeStruct((CHIPS, 8, 128), f32),
+        compiler_params=params(),
+        cost_estimate=cost(4 * KR * PACK, 1e6),
+    )(g, o, squares)
+
+
 RATES = (D ** (-0.5), max(1, 2 * D // S) ** (-0.5), D ** (-0.5), FF ** (-0.5), RATE_VECTOR)
 
 
-def adam_kernel(place_ref, norm_ref, mine_ref, other_ref, *refs):
+def adam_kernel(place_ref, norm_ref, mine_ref, other_ref, g1_ref, g2_ref, *refs):
     masters, firsts, seconds = refs[0:5], refs[5:10], refs[10:15]
     outs = refs[15:30]
     norm_out, bias_out = refs[30:32]
@@ -900,24 +979,17 @@
                 update(0, (rows, slice(col, col + 128)), g[:, (4 * p + i) * 128 : (4 * p + i + 1) * 128])
             col = c * DC + p * 128
             update(1, (rows, slice(col, col + 128)), g[:, (4 * p + 3) * 128 : (4 * p + 4) * 128])
-        base = 4 * DC + 128 + FC
-        for h in range(2):
-            row = c * FR + h * KR
-            update(3, (slice(row, row + KR), rows), g[:, base + h * D : base + (h + 1) * D])
-    base = 4 * DC + 128
-    for r in range(FC // DC):
-        at = slice(base + r * DC, base + (r + 1) * DC)
-        part = exact_dot(g0[:, at], spots_t(0)) + exact_dot(g1[:, at], spots_t(1))
-        update(2, (rows, slice(r * D, (r + 1) * D)), part)
+    update(2, (rows, rows), g1_ref[...])
+    update(3, (rows, rows), g2_ref[...])
     vec = (g0 + g1)[:, 4 * DC : 4 * DC + 128]
     vec = jnp.concatenate([vec, jnp.zeros((16 - KR, 128), f32)], axis=0).T[:16, :KR]
     update(4, (rows, rows), vec[: masters[4].shape[0], :])
     bias_out[...] = vec[7:8, :] * clip
 
 
-def adam_call(place, norm, mine, other, masters, firsts, seconds):
+def adam_call(place, norm, mine, other, g1, g2, masters, firsts, seconds):
     whole = lambda a: pl.BlockSpec(a.shape, lambda i, c: (0,) * len(a.shape))
-    args = [norm, mine, other, *masters, *firsts, *seconds]
+    args = [norm, mine, other, g1, g2, *masters, *firsts, *seconds]
     shapes = [jax.ShapeDtypeStruct(m.shape, f32) for m in masters for _ in range(3)]
     shapes += [jax.ShapeDtypeStruct((1, 128), f32), jax.ShapeDtypeStruct((1, KR), f32)]
     return pl.pallas_call(
@@ -985,16 +1057,15 @@
     parts = [halves(qkv_b[:, i * D : (i + 1) * D]) for i in range(3)]
     by_pair = [parts[i][:, p * 128 : (p + 1) * 128] for p in range(PAIRS) for i in range(3)]
     vec_t = jnp.pad(vectors.astype(bf16).T, ((0, 0), (0, 128 - vr)))
-    quarter = over_plane(jnp.concatenate(by_pair + [vec_t], axis=1))
-    vec_pieces = along_line(quarter[:, 3 * DC :])
-    qkv_pieces = along_line(quarter[:, : 3 * DC])
     fc1_b = w_fc1.astype(bf16).reshape(KR, CHIPS, CORES, FR)
     share_fc1 = jnp.where(first_core, fc1_b[:, :, 0], fc1_b[:, :, 1]).reshape(KR, FC)
-    share = jnp.concatenate([share_fc1, w_proj.astype(bf16)], axis=1)
-    share, vec_pieces = lax.optimization_barrier((share, vec_pieces))
-    quarter = over_plane(share)
-    proj_pieces = along_line(quarter[:, FC:])
-    fc1_pieces = along_line(quarter[:, :FC])
+    quarter = over_plane(jnp.concatenate(by_pair + [vec_t, w_proj.astype(bf16), share_fc1], axis=1))
+    cut = 3 * DC
+    qkv_pieces = along_line(quarter[:, :cut])
+    vec_pieces = along_line(quarter[:, cut : cut + 128])
+    quarter, vec_pieces = lax.optimization_barrier((quarter, vec_pieces))
+    proj_pieces = along_line(quarter[:, cut + 128 : cut + 128 + D])
+    fc1_pieces = along_line(quarter[:, cut + 128 + D :])
 
     x_own = tokens.reshape(S, D)
     cot_own = cotangent.reshape(S, D)
@@ -1012,42 +1083,44 @@
     counts1 = jnp.where(first_core, ints[1, 2, :1], ints[0, 2, :1])
     place = jnp.concatenate([jnp.stack([core, along]).astype(jnp.int32), counts0, counts1])
 
-    vec, h1, h1t, cosine, sine, gy, b1, pos = pre_call(place, x_own, x_other, cot_own, cot_other, ints, vec_pieces)
+    gy = gy_call(place, cot_own, cot_other)
+    vec, h1, h1t, cosine, sine, b1, pos = pre_call(place, x_own, x_other, ints, vec_pieces)
     q, k, v = qkv_call(place, h1, qkv_pieces, vec, cosine, sine)
     mine, p0, p1 = attn_fwd_call(place, q, k, v)
     other = swap(mine)
     after, h2 = proj_call(place, mine, other, x_own, x_other, proj_pieces, vec)
-    mlp, mlp_part, gh2, act, gup, gb1 = mlp_call(place, h2, gy, fc1_pieces, full_fc2, b1)
+    mlp, mlp_part, act, slope = mlp_call(place, h2, fc1_pieces, full_fc2, b1)
     mlp_other = swap(mlp_part)
+
+    sum_fc2 = line_sum(fc2_grad_call(place, act, gy))
+    gh2, gup, gb1 = mlp_back_call(place, gy, slope, fc1_pieces, full_fc2)
     other_gh2 = swap(gh2)
-
-    gw1, gw2 = fc_grad_call(place, h2, gup, act, gy)
-    sum_fc2 = line_sum(gw2)
-    sum_fc1 = line_sum(gw1)
+    sum_fc1 = line_sum(fc1_grad_call(place, h2, gup))
     ga, gab, sums_mid = mid_call(place, after, gy, gh2, other_gh2, vec)
-    *gw, gh1, gh1_part, sums_att = attn_bwd_call(
-        place, q, k, v, gab, mine, other, p0, p1, cosine, sine, pos, h1t, qkv_pieces, proj_pieces
+    gab, sum_fc2 = lax.optimization_barrier((gab, sum_fc2))
+    got_fc2 = plane_swap(sum_fc2.reshape(PLANE, FR, D))
+    *gw, gh1, gh1_part = attn_bwd_call(
+        place, q, k, v, gab, mine, other, p0, p1, cosine, sine, pos, h1t, qkv_pieces, proj_pieces,
+        x_own, x_other, sums_mid, gb1,
     )
     gh1_other = swap(gh1_part)
-
-    sums_qkv = [gw[0]] + [shift(gw[d], d) for d in range(1, SIDE)]
-    vec_parts = vec_call(place, x_own, x_other, gh1, gh1_part, sums_mid, sums_att, gb1)
-    sums_vec = [vec_parts[0]] + [shift(vec_parts[d], d) for d in range(1, SIDE)]
-    grads = sum_call(plane_swap(pack_call(sums_qkv, sums_vec, sum_fc1, sum_fc2)))
+    got_fc1 = plane_swap(sum_fc1.reshape(PLANE, KR, FC))
+
+    parts = [gw[0]] + [shift(gw[d], d) for d in range(1, SIDE)]
+    g_fc2, g_fc1 = sum_call(got_fc2), sum_call(got_fc1)
+    g1, g2, squares = fc_call(place, g_fc1, swap(g_fc1), g_fc2, swap(g_fc2))
+    grads = sum_call(plane_swap(pack_call(parts)))
     gt, mixed = last_call(x_own, ga, gh1, gh1_other, after, mlp, mlp_other, vec)
 
     grads_other = swap(grads)
-    is_vec = (jnp.arange(PACK) >= 4 * DC) & (jnp.arange(PACK) < 4 * DC + 128)
-    squares = jnp.where(
-        is_vec, (grads + grads_other) * (grads + grads_other), grads * grads + grads_other * grads_other
-    )
-    squares = jnp.sum(squares)
-    norms = lax.all_to_all(jnp.full((CHIPS, 8, 128), squares, f32), "dp", 0, 0)
+    norms = lax.all_to_all(norm_call(grads, grads_other, squares), "dp", 0, 0)
     *updates, grad_norm, bias_proj_grad = adam_call(
         place,
         norms,
         grads,
         grads_other,
+        g1,
+        g2,
         (w_qkv, w_proj, w_fc1, w_fc2, vectors),
         (m_qkv, m_proj, m_fc1, m_fc2, m_vectors),
         (v_qkv, v_proj, v_fc1, v_fc2, v_vectors),

time: 307 us -> 348 us (1.13)
  blocking collectives: 0 us -> 18 us
  Pallas kernels: 132 us -> 148 us
  waiting for transfers between devices: 76.5 us -> 84.1 us
  starting transfers between devices: 54 us -> 50.5 us
    pallas_call x3 -> x9, Pallas kernels: 21.9 us -> 42.5 us  [the longest x1 11.5 us: mlp_back_call(): pl.pallas_call(mlp_back_kernel, grid_spec=pltpu.PrefetchScalarGridSpec(nu...]
    reduce_scatter x2, waiting for transfers between devices: 0.04 us -> 19 us  [line_sum(): lax.psum_scatter(whole, BOTH, scatter_dimension=0, axis_index_groups=line...]
    all_to_all x0 -> x1, blocking collectives: none -> 18 us  [local(): norms = lax.all_to_all(norm_call(grads, grads_other, squares), 'dp', 0, 0)]
    all_to_all x3 -> x4, starting transfers between devices: 20.5 us -> 28.2 us  [plane_swap(): return lax.all_to_all(value, BOTH, 0, 0, axis_index_groups=planes())]
    all_to_all x1 -> x0, starting transfers between devices: 7.19 us -> none  [local(): norms = lax.all_to_all(jnp.full((CHIPS, 8, 128), squares, f32), 'dp', 0, 0)]
    all_to_all x1 -> x0, waiting for transfers between devices: 4.71 us -> none  [local(): norms = lax.all_to_all(jnp.full((CHIPS, 8, 128), squares, f32), 'dp', 0, 0)]
    ppermute x18 -> x15, starting transfers between devices: 24.4 us -> 20 us  [shift(): return lax.ppermute(value, BOTH, pairs)]
    pallas_call x1, Pallas kernels: 18.6 us -> 14.3 us  [mlp_call(): pl.pallas_call(mlp_kernel, grid_spec=pltpu.PrefetchScalarGridSpec(num_sca...]
  transfers between devices with their start and end apart: 33 -> 32, of which waited for: 10 -> 11; matrix products, arithmetic and copies ran while one was open for 4% -> 4% of each run, Pallas kernels for 30% -> 32%
where the time goes in v1:
time: 348 us; the launch traced here: 342 us
  Pallas kernels  148 us (43%)
  waiting for transfers between devices  84.1 us (24%)
  starting transfers between devices  50.5 us (15%)
  local copies, waits for them, and re-layouts  19.3 us (6%)
  blocking collectives  18 us (5%)
  between operations  15.8 us (5%)
  other arithmetic  6.14 us (2%)
    pallas_call x1, Pallas kernels, attn_bwd_call(): pl.pallas_call(attn_bwd_kernel, grid_spec=pltpu.PrefetchScalarGridSpec(nu...  33.1 us
    all_to_all x4, waiting for transfers between devices, plane_swap(): return lax.all_to_all(value, BOTH, 0, 0, axis_index_groups=planes())  31 us
    ppermute x15, waiting for transfers between devices, shift(): return lax.ppermute(value, BOTH, pairs)  28.4 us
    all_to_all x4, starting transfers between devices, plane_swap(): return lax.all_to_all(value, BOTH, 0, 0, axis_index_groups=planes())  28.2 us
    ppermute x15, starting transfers between devices, shift(): return lax.ppermute(value, BOTH, pairs)  20 us
    reduce_scatter x2, waiting for transfers between devices, line_sum(): lax.psum_scatter(whole, BOTH, scatter_dimension=0, axis_index_groups=line...  19 us
    all_to_all x1, blocking collectives, local(): norms = lax.all_to_all(norm_call(grads, grads_other, squares), 'dp', 0, 0)  18 us
    pallas_call x1, Pallas kernels, mlp_call(): pl.pallas_call(mlp_kernel, grid_spec=pltpu.PrefetchScalarGridSpec(num_sca...  14.3 us
  transfers between devices with their start and end apart: 32, of which 11 were waited for; matrix products, arithmetic and copies ran while one was open for 4% of the time, Pallas kernels for 32%

profile of v1, /device:TPU:0, one launch (start us, length us, event | category | flops | bytes accessed | tf_op | source)
XLA Modules:
  0.0 341.8 jit_solution(13529925651401297736)
XLA Ops:
  11.4 1.4 fusion
  13.3 1.4 broadcast_in_dim.10
  14.7 8.3 %all-to-all-start = ((bf16[16,12,3584]{2,1,0:T(8,128)(2,1)}), bf16[16,12,3584]{2,1,0:T(8,128)(2,1)S(1)}, u32[]{:S(2)}, u32[]{:S(2)}) async-start(bf16[16,12,3584]{2,1,0:T(8,128)(2,1)} %broadcast_in_dim.10), calls=%async_computation | async-start | bytes 3670016 | tf_op jit(solution)/shard_map/all_to_all | solution.py:74
  23.3 22.9 %all-to-all-done = bf16[16,12,3584]{2,1,0:T(8,128)(2,1)S(1)} async-done(((bf16[16,12,3584]{2,1,0:T(8,128)(2,1)}), bf16[16,12,3584]{2,1,0:T(8,128)(2,1)S(1)}, u32[]{:S(2)}, u32[]{:S(2)}) %all-to-all-start) | async-done | bytes 1376288 | tf_op jit(solution)/shard_map/all_to_all | solution.py:74
  46.2 1.3 reshape.109
  48.4 2.7 collective-permute-start.4
  53.4 1.0 slice.143.w0
  54.5 2.5 collective-permute-start.7
  57.0 1.5 collective-permute-start.6
  62.3 9.9 %shard_map.339 = (f32[16,768]{1,0:T(8,128)}, bf16[1152,768]{1,0:T(8,128)(2,1)}, bf16[2,768,576]{2,1,0:T(8,128)(2,1)}, f32[1152,384]{1,0:T(8,128)}, f32[1152,384]...) custom-call(s32[5]{0:T(128)} %pad_add_fusion.2.place_ref, bf16[576,768]{1,0:T(8,128)(2,1)} %bitcast.42, ...), custom_call_target="tpu_custom_call" | custom-call | flops 35389440 | bytes 12386304 | tf_op jit(solution)/shard_map/pallas_call | solution.py:270
  73.6 8.1 %shard_map.340 = (bf16[1152,384]{1,0:T(8,128)(2,1)}, bf16[1152,384]{1,0:T(8,128)(2,1)}, bf16[1152,384]{1,0:T(8,128)(2,1)}) custom-call(s32[5]{0:T(128)} %pad_add_fusion.2.place_ref, bf16[1152,768]{1,0:T(8,128)(2,1)} %get-tuple-element.83.h_ref, bf16[192,1152]{1,0:T(8,128)(2,1)} %copy-done.5, bf16[192,1152]{1,0:T(8,128)(2,1)} %copy-done.17, ...), custom_call_target="tpu_custom_call" | custom-call | flops 2038431744 | bytes 9732096 | tf_op jit(solution)/shard_map/pallas_call | solution.py:324
  81.7 11.4 %shard_map.341 = (bf16[2,576,384]{2,1,0:T(8,128)(2,1)}, bf16[6,2,208,208]{3,2,1,0:T(8,128)(2,1)}, bf16[6,576,576]{2,1,0:T(8,128)(2,1)}) custom-call(s32[5]{0:T(128)} %pad_add_fusion.2.place_ref, bf16[2,576,384]{2,1,0:T(8,128)(2,1)} %bitcast.30, bf16[2,576,384]{2,1,0:T(8,128)(2,1)} %bitcast.34, bf16[2,576,384]{2,1,0:T(8,128)(2,1)} %bitcast.38, ...), custom_call_target="tpu_custom_call" | custom-call | flops 1285029888 | bytes 12000000 | tf_op jit(solution)/shard_map/pallas_call | solution.py:380
  93.3 2.9 collective-permute-start.11
  97.1 1.1 collective-permute-start.15
  98.2 1.7 collective-permute-start.14
  99.9 3.7 %collective-permute-done.11.w3.y3 = bf16[192,768]{1,0:T(8,128)(2,1)S(1)} collective-permute-done((bf16[192,768]{1,0:T(8,128)(2,1)S(1)}, bf16[192,768]{1,0:T(8,128)(2,1)S(1)}, u32[]{:S(2)}, u32[]{:S(2)}) %collective-permute-start.11) | collective-permute-done | bytes 294944 | tf_op jit(solution)/shard_map/ppermute | solution.py:70
  105.3 3.6 %shard_map.343.gy_ref = bf16[1152,768]{1,0:T(8,128)(2,1)} custom-call(s32[5]{0:T(128)} %pad_add_fusion.2.place_ref, bf16[576,768]{1,0:T(8,128)(2,1)} %bitcast.54, bf16[576,768]{1,0:T(8,128)(2,1)} %copy-done.10), custom_call_target="tpu_custom_call" | custom-call | flops 3538944 | bytes 3538944 | tf_op jit(solution)/shard_map/pallas_call | solution.py:253
  108.8 11.3 %collective-permute-done.9.w1.y1 = bf16[192,768]{1,0:T(8,128)(2,1)S(1)} collective-permute-done((bf16[192,768]{1,0:T(8,128)(2,1)S(1)}, bf16[192,768]{1,0:T(8,128)(2,1)S(1)}, u32[]{:S(2)}, u32[]{:S(2)}) %collective-permute-start.9) | collective-permute-done | bytes 294944 | tf_op jit(solution)/shard_map/ppermute | solution.py:70
  121.8 7.8 %shard_map.342 = (f32[1152,768]{1,0:T(8,128)}, bf16[1152,768]{1,0:T(8,128)(2,1)}) custom-call(s32[5]{0:T(128)} %pad_add_fusion.2.place_ref, bf16[2,576,384]{2,1,0:T(8,128)(2,1)} %get-tuple-element.90.mine_ref.o0.o1, bf16[2,576,384]{2,1,0:T(8,128)(2,1)} %copy-done.9, bf16[576,768]{1,0:T(8,128)(2,1)} %bitcast.43, ...), custom_call_target="tpu_custom_call" | custom-call | flops 1358954496 | bytes 10027008 | tf_op jit(solution)/shard_map/pallas_call | solution.py:422
  131.3 14.3 %shard_map.344 = (f32[576,768]{1,0:T(8,128)}, f32[576,768]{1,0:T(8,128)}, bf16[1152,1536]{1,0:T(8,128)(2,1)}, bf16[1152,1536]{1,0:T(8,128)(2,1)}) custom-call(s32[5]{0:T(128)} %pad_add_fusion.2.place_ref, bf16[1152,768]{1,0:T(8,128)(2,1)} %get-tuple-element.93.h2_ref, bf16[192,1536]{1,0:T(8,128)(2,1)} %copy-done.14, ...), custom_call_target="tpu_custom_call" | custom-call | flops 5435817984 | bytes 20000000 | tf_op jit(solution)/shard_map/pallas_call | solution.py:487
  145.6 11.5 %shard_map.345 = (bf16[1152,768]{1,0:T(8,128)(2,1)}, bf16[1152,1536]{1,0:T(8,128)(2,1)}, f32[1,1536]{1,0:T(1,128)}) custom-call(s32[5]{0:T(128)} %pad_add_fusion.2.place_ref, bf16[1152,768]{1,0:T(8,128)(2,1)} %shard_map.343.gy_ref, bf16[1152,1536]{1,0:T(8,128)(2,1)} %get-tuple-element.95.slope_ref, bf16[192,1536]{1,0:T(8,128)(2,1)} %copy-done.14, ...), custom_call_target="tpu_custom_call" | custom-call | flops 5435817984 | bytes 16000000 | tf_op jit(solution)/shard_map/pallas_call | solution.py:530
  157.0 7.3 %shard_map.352 = bf16[768,1536]{1,0:T(8,128)(2,1)} custom-call(s32[5]{0:T(128)} %pad_add_fusion.2.place_ref, bf16[1152,768]{1,0:T(8,128)(2,1)} %get-tuple-element.93.h2_ref, bf16[1152,1536]{1,0:T(8,128)(2,1)} %get-tuple-element.117.gup_ref), custom_call_target="tpu_custom_call" | custom-call | flops 2717908992 | bytes 7667712 | tf_op jit(solution)/shard_map/pallas_call | solution.py:561
  164.4 8.3 %shard_map.347 = bf16[1536,768]{1,0:T(8,128)(2,1)} custom-call(s32[5]{0:T(128)} %pad_add_fusion.2.place_ref, bf16[1152,1536]{1,0:T(8,128)(2,1)} %get-tuple-element.103.act_ref, bf16[1152,768]{1,0:T(8,128)(2,1)} %shard_map.343.gy_ref), custom_call_target="tpu_custom_call" | custom-call | flops 2717908992 | bytes 7667712 | tf_op jit(solution)/shard_map/pallas_call | solution.py:580
  172.7 1.4 copy-done.6
  174.7 5.7 %collective-permute-done.16.other_ref = bf16[1152,768]{1,0:T(8,128)(2,1)S(1)} collective-permute-done((bf16[1152,768]{1,0:T(8,128)(2,1)S(1)}, bf16[1152,768]{1,0:T(8,128)(2,1)S(1)}, u32[]{:S(2)}, u32[]{:S(2)}) %collective-permute-start.16) | collective-permute-done | bytes 1769504 | tf_op jit(solution)/shard_map/ppermute | solution.py:1038
  180.4 1.2 copy-done.7
  181.6 8.2 %shard_map.346 = (f32[576,768]{1,0:T(8,128)}, bf16[1152,768]{1,0:T(8,128)(2,1)}, f32[8,768]{1,0:T(8,128)}) custom-call(s32[5]{0:T(128)} %pad_add_fusion.2.place_ref, f32[1152,768]{1,0:T(8,128)} %get-tuple-element.92.after_ref, bf16[1152,768]{1,0:T(8,128)(2,1)} %shard_map.343.gy_ref, bf16[1152,768]{1,0:T(8,128)(2,1)} %get-tuple-element.96.gh2_ref, ...), custom_call_target="tpu_custom_call" | custom-call | flops 26542080 | bytes 12386304 | tf_op jit(solution)/shard_map/pallas_call | solution.py:622
  189.8 2.1 reshape.119
  191.8 6.6 %all-to-all-start.2 = ((bf16[16,12,1536]{2,1,0:T(8,128)(2,1)}), bf16[16,12,1536]{2,1,0:T(8,128)(2,1)S(1)}, u32[]{:S(2)}, u32[]{:S(2)}) async-start(bf16[16,12,1536]{2,1,0:T(8,128)(2,1)} %reshape.119), calls=%async_computation.4 | async-start | bytes 1572864 | tf_op jit(solution)/shard_map/all_to_all | solution.py:74
  198.4 19.0 %reduce-scatter.3.cloned.1.call-done = bf16[384,768]{1,0:T(8,128)(2,1)} async-done(((bf16[1536,768]{1,0:T(8,128)(2,1)}), bf16[384,768]{1,0:T(8,128)(2,1)}) %reduce-scatter.3.cloned.1.call-update) | async-done | bytes 589840 | tf_op jit(solution)/shard_map/reduce_scatter | solution.py:1052
  217.4 33.1 %shard_map.348 = (bf16[192,1664]{1,0:T(8,128)(2,1)}, bf16[192,1664]{1,0:T(8,128)(2,1)}, bf16[192,1664]{1,0:T(8,128)(2,1)}, bf16[192,1664]{1,0:T(8,128)(2,1)}, f32[576,768]{1,0:T(8,128)}, /*index=5*/f32[576,768]{1,0:T(8,128)}) custom-call(s32[5]{0:T(128)} %pad_add_fusion.2.place_ref, bf16[2,576,384]{2,1,0:T(8,128)(2,1)} %bitcast.32, ...), custom_call_target="tpu_custom_call" | custom-call | flops 7983857664 | bytes 36000000 | tf_op jit(solution)/shard_map/pallas_call | solution.py:805
  250.7 2.9 collective-permute-start.20
  253.6 1.2 collective-permute-start.21
  254.8 6.7 %all-to-all-start.3 = ((bf16[16,24,768]{2,1,0:T(8,128)(2,1)}), bf16[16,24,768]{2,1,0:T(8,128)(2,1)S(1)}, u32[]{:S(2)}, u32[]{:S(2)}) async-start(bf16[16,24,768]{2,1,0:T(8,128)(2,1)} %bitcast.55), calls=%async_computation.5 | async-start | bytes 1179648 | tf_op jit(solution)/shard_map/all_to_all | solution.py:74
  261.5 4.5 %collective-permute-done.19.q1 = bf16[192,1664]{1,0:T(8,128)(2,1)S(1)} collective-permute-done((bf16[192,1664]{1,0:T(8,128)(2,1)}, bf16[192,1664]{1,0:T(8,128)(2,1)S(1)}, u32[]{:S(2)}, u32[]{:S(2)}) %collective-permute-start.19) | collective-permute-done | bytes 639008 | tf_op jit(solution)/shard_map/ppermute | solution.py:70
  266.0 6.2 %collective-permute-done.20.q2 = bf16[192,1664]{1,0:T(8,128)(2,1)S(1)} collective-permute-done((bf16[192,1664]{1,0:T(8,128)(2,1)}, bf16[192,1664]{1,0:T(8,128)(2,1)S(1)}, u32[]{:S(2)}, u32[]{:S(2)}) %collective-permute-start.20) | collective-permute-done | bytes 639008 | tf_op jit(solution)/shard_map/ppermute | solution.py:70
  272.2 1.2 collective-permute-done.21.q3
  274.2 2.9 shard_map.350
  277.2 6.7 %all-to-all-start.1 = ((bf16[16,12,1664]{2,1,0:T(8,128)(2,1)}), bf16[16,12,1664]{2,1,0:T(8,128)(2,1)S(1)}, u32[]{:S(2)}, u32[]{:S(2)}) async-start(bf16[16,12,1664]{2,1,0:T(8,128)(2,1)} %shard_map.350), calls=%async_computation.2 | async-start | bytes 1703936 | tf_op jit(solution)/shard_map/all_to_all | solution.py:74
  283.9 1.9 shard_map.353.f1_ref
  285.8 1.8 shard_map.354.f2_ref
  288.2 8.1 %all-to-all-done.1.in_ref = bf16[16,12,1664]{2,1,0:T(8,128)(2,1)S(1)} async-done(((bf16[16,12,1664]{2,1,0:T(8,128)(2,1)}), bf16[16,12,1664]{2,1,0:T(8,128)(2,1)S(1)}, u32[]{:S(2)}, u32[]{:S(2)}) %all-to-all-start.1) | async-done | bytes 639008 | tf_op jit(solution)/shard_map/all_to_all | solution.py:74
  297.2 1.9 shard_map.351.g_ref.mine_ref
  300.3 4.4 %shard_map.355 = (f32[12,3072]{1,0:T(8,128)}, f32[48,768]{1,0:T(8,128)}, f32[8,128]{1,0:T(8,128)}) custom-call(s32[5]{0:T(128)} %pad_add_fusion.2.place_ref, f32[12,1536]{1,0:T(8,128)} %shard_map.353.f1_ref, f32[12,1536]{1,0:T(8,128)} %copy-done.33, f32[24,768]{1,0:T(8,128)} %shard_map.354.f2_ref, f32[24,768]{1,0:T(8,128)} %copy-done.34), custom_call_target="tpu_custom_call" | custom-call | flops 169869312 | bytes 1000000 | tf_op jit(solution)/shard_map/pallas_call | solution.py:914
  305.4 1.8 shard_map.356
  307.2 18.0 %all_to_all.25.norm_ref = f32[64,8,128]{2,1,0:T(8,128)} all-to-all(f32[64,8,128]{2,1,0:T(8,128)} %shard_map.356), channel_id=1, replica_groups=mesh['grp'=2,'dp'=64] {'dp'}, dimensions={0} | all-to-all | bytes 524288 | tf_op jit(solution)/shard_map/all_to_all | solution.py:1116
  325.2 3.9 %shard_map.357 = (f32[12,2304]{1,0:T(8,128)}, f32[12,2304]{1,0:T(8,128)}, f32[12,2304]{1,0:T(8,128)}, f32[12,768]{1,0:T(8,128)}, f32[12,768]{1,0:T(8,128)}, /*in...) custom-call(s32[5]{0:T(128)} %pad_add_fusion.2.place_ref, ...), custom_call_target="tpu_custom_call" | custom-call | flops 2211840 | bytes 3000000 | tf_op jit(solution)/shard_map/pallas_call | solution.py:995
  329.1 6.0 %shard_map.349 = (f32[576,768]{1,0:T(8,128)}, bf16[576,768]{1,0:T(8,128)(2,1)}) custom-call(bf16[576,768]{1,0:T(8,128)(2,1)} %bitcast.45, f32[576,768]{1,0:T(8,128)} %get-tuple-element.97.ga_ref, f32[576,768]{1,0:T(8,128)} %get-tuple-element.107.gh_ref, f32[576,768]{1,0:T(8,128)} %collective-permute-done.17.other_ref, ...), custom_call_target="tpu_custom_call" | custom-call | flops 13271040 | bytes 12386304 | tf_op jit(solution)/shard_map/pallas_call | solution.py:854
  (145 shorter events, 22.9 us)
Async XLA Ops:
  7.2 5.7 %copy-start.27 = (f32[14,12]{1,0:T(8,128)S(1)}, f32[14,12]{1,0:T(8,128)}, u32[]{:S(2)}) copy-start(f32[14,12]{1,0:T(8,128)} %refs_4_.1) | copy-start | bytes 2020
  7.2 6.1 %copy-start.22 = (f32[12,768]{1,0:T(8,128)S(1)}, f32[12,768]{1,0:T(8,128)}, u32[]{:S(2)}) copy-start(f32[12,768]{1,0:T(8,128)} %refs_1_.1) | copy-start | bytes 110596
  7.2 124.0 %all-gather.2.cloned.1.call-start = ((), (), s32[]{:S(2)}) async-start(), calls=%async_computation.7 | async-start | bytes 2396160 | tf_op jit(solution)/shard_map/all_gather | solution.py:1055
  14.7 8.4 %copy-start = (bf16[1,1,576,768]{3,2,1,0:T(8,128)(2,1)S(1)}, bf16[1,1,576,768]{3,2,1,0:T(8,128)(2,1)}, u32[]{:S(2)}) copy-start(bf16[1,1,576,768]{3,2,1,0:T(8,128)(2,1)} %param.20) | copy-start | bytes 2654212
  14.7 31.5 %all-to-all-start = ((bf16[16,12,3584]{2,1,0:T(8,128)(2,1)}), bf16[16,12,3584]{2,1,0:T(8,128)(2,1)S(1)}, u32[]{:S(2)}, u32[]{:S(2)}) async-start(bf16[16,12,3584]{2,1,0:T(8,128)(2,1)} %broadcast_in_dim.10), calls=%async_computation | async-start | bytes 3670016 | tf_op jit(solution)/shard_map/all_to_all | solution.py:74
  23.0 28.9 %copy-start.28 = (s32[1,1,576]{2,1,0:T(1,128)S(1)}, s32[1,1,576]{2,1,0:T(1,128)}, u32[]{:S(2)}) copy-start(s32[1,1,576]{2,1,0:T(1,128)} %param.24) | copy-start | bytes 6916
  23.0 28.9 %copy-start.29 = (s32[1,1,576]{2,1,0:T(1,128)S(1)}, s32[1,1,576]{2,1,0:T(1,128)}, u32[]{:S(2)}) copy-start(s32[1,1,576]{2,1,0:T(1,128)} %param.23) | copy-start | bytes 6916
  23.0 28.9 %copy-start.30 = (s32[1,1,2]{2,1,0:T(1,128)S(1)}, s32[1,1,2]{2,1,0:T(1,128)}, u32[]{:S(2)}) copy-start(s32[1,1,2]{2,1,0:T(1,128)} %param.22) | copy-start | bytes 28
  23.0 166.7 %reduce-scatter.5.cloned.1.call-start = ((), (), s32[]{:S(2)}) async-start(), calls=%async_computation.9 | async-start | bytes 2949120 | tf_op jit(solution)/shard_map/reduce_scatter | solution.py:1052
  23.1 39.2 %collective-permute-start.1 = (bf16[576,768]{1,0:T(8,128)(2,1)S(1)}, bf16[576,768]{1,0:T(8,128)(2,1)}, u32[]{:S(2)}, u32[]{:S(2)}) collective-permute-start(bf16[576,768]{1,0:T(8,128)(2,1)S(1)} %bitcast.46), channel_id=1, source_target_pairs={{0,64},{64,0},{1,65},{65,1},{2,66},{66,2},{3,67},{67,3},{4,68},{68... | collective-permute-start | bytes 2654216 | tf_op jit(solution)/shard_map/ppermute | solution.py:1038
  48.4 13.9 %copy-start.23 = (bf16[192,128]{1,0:T(8,128)(2,1)}, bf16[192,128]{1,0:T(8,128)(2,1)S(1)}, u32[]{:S(2)}) copy-start(bf16[192,128]{1,0:T(8,128)(2,1)S(1)} %slice.142.v0) | copy-start | bytes 147460
  48.4 8.6 %collective-permute-start.4 = (bf16[192,128]{1,0:T(8,128)(2,1)S(1)}, bf16[192,128]{1,0:T(8,128)(2,1)S(1)}, u32[]{:S(2)}, u32[]{:S(2)}) collective-permute-start(bf16[192,128]{1,0:T(8,128)(2,1)S(1)} %slice.142.v0), channel_id=1, source_target_pairs={{0,48},{16,0},{32,16},{48,32},{1,49},{17,1},{33,17},{49,33},{2,50}... | collective-permute-start | bytes 147464 | tf_op jit(solution)/shard_map/ppermute | solution.py:70
  51.1 7.4 %collective-permute-start.3 = (bf16[192,128]{1,0:T(8,128)(2,1)S(1)}, bf16[192,128]{1,0:T(8,128)(2,1)S(1)}, u32[]{:S(2)}, u32[]{:S(2)}) collective-permute-start(bf16[192,128]{1,0:T(8,128)(2,1)S(1)} %slice.142.v0), channel_id=1, source_target_pairs={{0,32},{16,48},{32,0},{48,16},{1,33},{17,49},{33,1},{49,17},{2,34}... | collective-permute-start | bytes 147464 | tf_op jit(solution)/shard_map/ppermute | solution.py:70
  52.0 2.5 collective-permute-start
  52.6 7.7 %collective-permute-start.2 = (bf16[192,128]{1,0:T(8,128)(2,1)S(1)}, bf16[192,128]{1,0:T(8,128)(2,1)S(1)}, u32[]{:S(2)}, u32[]{:S(2)}) collective-permute-start(bf16[192,128]{1,0:T(8,128)(2,1)S(1)} %slice.142.v0), channel_id=1, source_target_pairs={{0,16},{16,32},{32,48},{48,0},{1,17},{17,33},{33,49},{49,1},{2,18}... | collective-permute-start | bytes 147464 | tf_op jit(solution)/shard_map/ppermute | solution.py:70
  54.5 18.4 %copy-start.5 = (bf16[192,1152]{1,0:T(8,128)(2,1)}, bf16[192,1152]{1,0:T(8,128)(2,1)S(1)}, u32[]{:S(2)}) copy-start(bf16[192,1152]{1,0:T(8,128)(2,1)S(1)} %slice.143.w0) | copy-start | bytes 1327108
  54.5 17.7 %collective-permute-start.7 = (bf16[192,1152]{1,0:T(8,128)(2,1)S(1)}, bf16[192,1152]{1,0:T(8,128)(2,1)S(1)}, u32[]{:S(2)}, u32[]{:S(2)}) collective-permute-start(bf16[192,1152]{1,0:T(8,128)(2,1)S(1)} %slice.143.w0), channel_id=1, source_target_pairs={{0,48},{16,0},{32,16},{48,32},{1,49},{17,1},{33,17},{49,33},{2,50}... | collective-permute-start | bytes 1327112 | tf_op jit(solution)/shard_map/ppermute | solution.py:70
  57.0 5.3 %copy-start.24 = (bf16[192,128]{1,0:T(8,128)(2,1)}, bf16[192,128]{1,0:T(8,128)(2,1)S(1)}, u32[]{:S(2)}) copy-start(bf16[192,128]{1,0:T(8,128)(2,1)S(1)} %collective-permute-done.4.v3) | copy-start | bytes 147460
  57.0 15.2 %collective-permute-start.6 = (bf16[192,1152]{1,0:T(8,128)(2,1)S(1)}, bf16[192,1152]{1,0:T(8,128)(2,1)S(1)}, u32[]{:S(2)}, u32[]{:S(2)}) collective-permute-start(bf16[192,1152]{1,0:T(8,128)(2,1)S(1)} %slice.143.w0), channel_id=1, source_target_pairs={{0,32},{16,48},{32,0},{48,16},{1,33},{17,49},{33,1},{49,17},{2,34}... | collective-permute-start | bytes 1327112 | tf_op jit(solution)/shard_map/ppermute | solution.py:70
  58.4 14.4 %collective-permute-start.5 = (bf16[192,1152]{1,0:T(8,128)(2,1)S(1)}, bf16[192,1152]{1,0:T(8,128)(2,1)S(1)}, u32[]{:S(2)}, u32[]{:S(2)}) collective-permute-start(bf16[192,1152]{1,0:T(8,128)(2,1)S(1)} %slice.143.w0), channel_id=1, source_target_pairs={{0,16},{16,32},{32,48},{48,0},{1,17},{17,33},{33,49},{49,1},{2,18}... | collective-permute-start | bytes 1327112 | tf_op jit(solution)/shard_map/ppermute | solution.py:70
  60.3 37.9 %collective-permute-start.12 = (bf16[576,768]{1,0:T(8,128)(2,1)}, bf16[576,768]{1,0:T(8,128)(2,1)S(1)}, u32[]{:S(2)}, u32[]{:S(2)}) collective-permute-start(bf16[576,768]{1,0:T(8,128)(2,1)} %bitcast.53), channel_id=1, source_target_pairs={{0,64},{64,0},{1,65},{65,1},{2,66},{66,2},{3,67},{67,3},{4,68},{68... | collective-permute-start | bytes 2654216 | tf_op jit(solution)/shard_map/ppermute | solution.py:1038
  81.7 11.5 %copy-start.1 = (bf16[192,3584]{1,0:T(8,128)(2,1)S(1)}, bf16[192,3584]{1,0:T(8,128)(2,1)}, u32[]{:S(2)}) copy-start(bf16[192,3584]{1,0:T(8,128)(2,1)} %reshape.109) | copy-start | bytes 4128772
  93.2 27.0 %collective-permute-start.8 = (bf16[2,576,384]{2,1,0:T(8,128)(2,1)}, bf16[2,576,384]{2,1,0:T(8,128)(2,1)S(1)}, u32[]{:S(2)}, u32[]{:S(2)}) collective-permute-start(bf16[2,576,384]{2,1,0:T(8,128)(2,1)} %get-tuple-element.90.mine_ref.o0.o1), channel_id=1, source_target_pairs={{0,64},{64,0},{1,65},{65,1},{2,66},{66,2},{3,67},{67,3},{4,68},{68... | collective-permute-start | bytes 2654216 | tf_op jit(solution)/shard_map/ppermute | solution.py:1038
  93.3 15.5 %copy-start.8 = (bf16[192,768]{1,0:T(8,128)(2,1)}, bf16[192,768]{1,0:T(8,128)(2,1)S(1)}, u32[]{:S(2)}) copy-start(bf16[192,768]{1,0:T(8,128)(2,1)S(1)} %slice.116.w0.y0) | copy-start | bytes 884740
  93.3 10.3 %collective-permute-start.11 = (bf16[192,768]{1,0:T(8,128)(2,1)S(1)}, bf16[192,768]{1,0:T(8,128)(2,1)S(1)}, u32[]{:S(2)}, u32[]{:S(2)}) collective-permute-start(bf16[192,768]{1,0:T(8,128)(2,1)S(1)} %slice.116.w0.y0), channel_id=1, source_target_pairs={{0,48},{16,0},{32,16},{48,32},{1,49},{17,1},{33,17},{49,33},{2,50}... | collective-permute-start | bytes 884744 | tf_op jit(solution)/shard_map/ppermute | solution.py:70
  96.2 8.2 %collective-permute-start.10 = (bf16[192,768]{1,0:T(8,128)(2,1)S(1)}, bf16[192,768]{1,0:T(8,128)(2,1)S(1)}, u32[]{:S(2)}, u32[]{:S(2)}) collective-permute-start(bf16[192,768]{1,0:T(8,128)(2,1)S(1)} %slice.116.w0.y0), channel_id=1, source_target_pairs={{0,32},{16,48},{32,0},{48,16},{1,33},{17,49},{33,1},{49,17},{2,34}... | collective-permute-start | bytes 884744 | tf_op jit(solution)/shard_map/ppermute | solution.py:70
  97.1 34.2 %copy-start.14 = (bf16[192,1536]{1,0:T(8,128)(2,1)}, bf16[192,1536]{1,0:T(8,128)(2,1)S(1)}, u32[]{:S(2)}) copy-start(bf16[192,1536]{1,0:T(8,128)(2,1)S(1)} %slice.117.w10) | copy-start | bytes 1769476
  97.1 32.6 %collective-permute-start.15 = (bf16[192,1536]{1,0:T(8,128)(2,1)S(1)}, bf16[192,1536]{1,0:T(8,128)(2,1)S(1)}, u32[]{:S(2)}, u32[]{:S(2)}) collective-permute-start(bf16[192,1536]{1,0:T(8,128)(2,1)S(1)} %slice.117.w10), channel_id=1, source_target_pairs={{0,48},{16,0},{32,16},{48,32},{1,49},{17,1},{33,17},{49,33},{2,50}... | collective-permute-start | bytes 1769480 | tf_op jit(solution)/shard_map/ppermute | solution.py:70
  98.2 7.1 %copy-start.10 = (bf16[576,768]{1,0:T(8,128)(2,1)}, bf16[576,768]{1,0:T(8,128)(2,1)S(1)}, u32[]{:S(2)}) copy-start(bf16[576,768]{1,0:T(8,128)(2,1)S(1)} %collective-permute-done.12.co_ref) | copy-start | bytes 2654212
  98.2 31.4 %collective-permute-start.14 = (bf16[192,1536]{1,0:T(8,128)(2,1)S(1)}, bf16[192,1536]{1,0:T(8,128)(2,1)S(1)}, u32[]{:S(2)}, u32[]{:S(2)}) collective-permute-start(bf16[192,1536]{1,0:T(8,128)(2,1)S(1)} %slice.117.w10), channel_id=1, source_target_pairs={{0,32},{16,48},{32,0},{48,16},{1,33},{17,49},{33,1},{49,17},{2,34}... | collective-permute-start | bytes 1769480 | tf_op jit(solution)/shard_map/ppermute | solution.py:70
  103.6 27.7 %collective-permute-start.13 = (bf16[192,1536]{1,0:T(8,128)(2,1)S(1)}, bf16[192,1536]{1,0:T(8,128)(2,1)}, u32[]{:S(2)}, u32[]{:S(2)}) collective-permute-start(bf16[192,1536]{1,0:T(8,128)(2,1)S(1)} %slice.117.w10), channel_id=1, source_target_pairs={{0,16},{16,32},{32,48},{48,0},{1,17},{17,33},{33,49},{49,1},{2,18}... | collective-permute-start | bytes 1769480 | tf_op jit(solution)/shard_map/ppermute | solution.py:70
  104.4 15.8 %collective-permute-start.9 = (bf16[192,768]{1,0:T(8,128)(2,1)S(1)}, bf16[192,768]{1,0:T(8,128)(2,1)S(1)}, u32[]{:S(2)}, u32[]{:S(2)}) collective-permute-start(bf16[192,768]{1,0:T(8,128)(2,1)S(1)} %slice.116.w0.y0), channel_id=1, source_target_pairs={{0,16},{16,32},{32,48},{48,0},{1,17},{17,33},{33,49},{49,1},{2,18}... | collective-permute-start | bytes 884744 | tf_op jit(solution)/shard_map/ppermute | solution.py:70
  164.3 53.1 %reduce-scatter.3.cloned.1.call-start = ((), (), s32[]{:S(2)}) async-start(), calls=%async_computation.8 | async-start | bytes 2949120 | tf_op jit(solution)/shard_map/reduce_scatter | solution.py:1052
  174.2 6.2 %collective-permute-start.16 = (bf16[1152,768]{1,0:T(8,128)(2,1)S(1)}, bf16[1152,768]{1,0:T(8,128)(2,1)S(1)}, u32[]{:S(2)}, u32[]{:S(2)}) collective-permute-start(bf16[1152,768]{1,0:T(8,128)(2,1)S(1)} %copy-done.6), channel_id=1, source_target_pairs={{0,64},{64,0},{1,65},{65,1},{2,66},{66,2},{3,67},{67,3},{4,68},{68... | collective-permute-start | bytes 5308424 | tf_op jit(solution)/shard_map/ppermute | solution.py:1038
  174.2 154.9 %collective-permute-start.18 = (f32[576,768]{1,0:T(8,128)}, f32[576,768]{1,0:T(8,128)}, u32[]{:S(2)}, u32[]{:S(2)}) collective-permute-start(f32[576,768]{1,0:T(8,128)} %get-tuple-element.110), channel_id=1, source_target_pairs={{0,64},{64,0},{1,65},{65,1},{2,66},{66,2},{3,67},{67,3},{4,68},{68... | collective-permute-start | bytes 5308424 | tf_op jit(solution)/shard_map/ppermute | solution.py:1038
  191.8 63.0 %all-to-all-start.2 = ((bf16[16,12,1536]{2,1,0:T(8,128)(2,1)}), bf16[16,12,1536]{2,1,0:T(8,128)(2,1)S(1)}, u32[]{:S(2)}, u32[]{:S(2)}) async-start(bf16[16,12,1536]{2,1,0:T(8,128)(2,1)} %reshape.119), calls=%async_computation.4 | async-start | bytes 1572864 | tf_op jit(solution)/shard_map/all_to_all | solution.py:74
  250.5 78.6 %collective-permute-start.17 = (f32[576,768]{1,0:T(8,128)}, f32[576,768]{1,0:T(8,128)}, u32[]{:S(2)}, u32[]{:S(2)}) collective-permute-start(f32[576,768]{1,0:T(8,128)} %get-tuple-element.108), channel_id=1, source_target_pairs={{0,64},{64,0},{1,65},{65,1},{2,66},{66,2},{3,67},{67,3},{4,68},{68... | collective-permute-start | bytes 5308424 | tf_op jit(solution)/shard_map/ppermute | solution.py:1038
  250.6 15.4 %collective-permute-start.19 = (bf16[192,1664]{1,0:T(8,128)(2,1)}, bf16[192,1664]{1,0:T(8,128)(2,1)S(1)}, u32[]{:S(2)}, u32[]{:S(2)}) collective-permute-start(bf16[192,1664]{1,0:T(8,128)(2,1)} %get-tuple-element.114), channel_id=1, source_target_pairs={{0,16},{16,32},{32,48},{48,0},{1,17},{17,33},{33,49},{49,1},{2,18}... | collective-permute-start | bytes 1916936 | tf_op jit(solution)/shard_map/ppermute | solution.py:70
  250.7 21.5 %collective-permute-start.20 = (bf16[192,1664]{1,0:T(8,128)(2,1)}, bf16[192,1664]{1,0:T(8,128)(2,1)S(1)}, u32[]{:S(2)}, u32[]{:S(2)}) collective-permute-start(bf16[192,1664]{1,0:T(8,128)(2,1)} %get-tuple-element.115), channel_id=1, source_target_pairs={{0,32},{16,48},{32,0},{48,16},{1,33},{17,49},{33,1},{49,17},{2,34}... | collective-permute-start | bytes 1916936 | tf_op jit(solution)/shard_map/ppermute | solution.py:70
  253.6 19.8 %collective-permute-start.21 = (bf16[192,1664]{1,0:T(8,128)(2,1)}, bf16[192,1664]{1,0:T(8,128)(2,1)S(1)}, u32[]{:S(2)}, u32[]{:S(2)}) collective-permute-start(bf16[192,1664]{1,0:T(8,128)(2,1)} %get-tuple-element.116), channel_id=1, source_target_pairs={{0,48},{16,0},{32,16},{48,32},{1,49},{17,1},{33,17},{49,33},{2,50}... | collective-permute-start | bytes 1916936 | tf_op jit(solution)/shard_map/ppermute | solution.py:70
  254.8 22.3 %copy-start.3 = (bf16[16,12,1536]{2,1,0:T(8,128)(2,1)}, bf16[16,12,1536]{2,1,0:T(8,128)(2,1)S(1)}, u32[]{:S(2)}) copy-start(bf16[16,12,1536]{2,1,0:T(8,128)(2,1)S(1)} %all-to-all-done.2.in_ref) | copy-start | bytes 1769476
  254.8 22.4 %all-to-all-start.3 = ((bf16[16,24,768]{2,1,0:T(8,128)(2,1)}), bf16[16,24,768]{2,1,0:T(8,128)(2,1)S(1)}, u32[]{:S(2)}, u32[]{:S(2)}) async-start(bf16[16,24,768]{2,1,0:T(8,128)(2,1)} %bitcast.55), calls=%async_computation.5 | async-start | bytes 1179648 | tf_op jit(solution)/shard_map/all_to_all | solution.py:74
  266.0 7.4 %copy-start.11 = (bf16[192,1664]{1,0:T(8,128)(2,1)}, bf16[192,1664]{1,0:T(8,128)(2,1)S(1)}, u32[]{:S(2)}) copy-start(bf16[192,1664]{1,0:T(8,128)(2,1)S(1)} %collective-permute-done.19.q1) | copy-start | bytes 1916932
  277.2 8.6 %copy-start.4 = (bf16[16,24,768]{2,1,0:T(8,128)(2,1)}, bf16[16,24,768]{2,1,0:T(8,128)(2,1)S(1)}, u32[]{:S(2)}) copy-start(bf16[16,24,768]{2,1,0:T(8,128)(2,1)S(1)} %all-to-all-done.3.in_ref) | copy-start | bytes 1769476
  277.2 19.1 %all-to-all-start.1 = ((bf16[16,12,1664]{2,1,0:T(8,128)(2,1)}), bf16[16,12,1664]{2,1,0:T(8,128)(2,1)S(1)}, u32[]{:S(2)}, u32[]{:S(2)}) async-start(bf16[16,12,1664]{2,1,0:T(8,128)(2,1)} %shard_map.350), calls=%async_computation.2 | async-start | bytes 1703936 | tf_op jit(solution)/shard_map/all_to_all | solution.py:74
  285.8 13.3 %collective-permute-start.23 = (f32[12,1536]{1,0:T(8,128)}, f32[12,1536]{1,0:T(8,128)S(1)}, u32[]{:S(2)}, u32[]{:S(2)}) collective-permute-start(f32[12,1536]{1,0:T(8,128)} %shard_map.353.f1_ref), channel_id=1, source_target_pairs={{0,64},{64,0},{1,65},{65,1},{2,66},{66,2},{3,67},{67,3},{4,68},{68... | collective-permute-start | bytes 221192 | tf_op jit(solution)/shard_map/ppermute | solution.py:1038
  287.5 11.5 %collective-permute-start.24 = (f32[24,768]{1,0:T(8,128)}, f32[24,768]{1,0:T(8,128)S(1)}, u32[]{:S(2)}, u32[]{:S(2)}) collective-permute-start(f32[24,768]{1,0:T(8,128)} %shard_map.354.f2_ref), channel_id=1, source_target_pairs={{0,64},{64,0},{1,65},{65,1},{2,66},{66,2},{3,67},{67,3},{4,68},{68... | collective-permute-start | bytes 221192 | tf_op jit(solution)/shard_map/ppermute | solution.py:1038
  299.1 5.7 %collective-permute-start.22 = (f32[12,1664]{1,0:T(8,128)}, f32[12,1664]{1,0:T(8,128)S(1)}, u32[]{:S(2)}, u32[]{:S(2)}) collective-permute-start(f32[12,1664]{1,0:T(8,128)} %shard_map.351.g_ref.mine_ref), channel_id=1, source_target_pairs={{0,64},{64,0},{1,65},{65,1},{2,66},{66,2},{3,67},{67,3},{4,68},{68... | collective-permute-start | bytes 239624 | tf_op jit(solution)/shard_map/ppermute | solution.py:1038
  (19 other events, 28.8 us)
Sparse Core Ops, SparseCore 0:
  11.5 86.2 all-gather.1
  164.4 23.5 reduce-scatter.4
  190.5 26.9 reduce-scatter.2
